TPU v7x, 32 devices: a whole 2x2x4 slice. The times are simulated.
32 devices in a mesh: dp: 8 (over z, core), ctx: 4 (over y, x).
Axes of the slice: x: 2, y: 2, z: 4, core: 2. Of those that a mesh axis runs over, the one named last changes fastest.
Arguments:
- hidden_in: bfloat16 [8, 1536, 896], P('dp', 'ctx'), may hold values from -6 to 6
- doc_start: int32 [8, 1536], P('dp', 'ctx'), may hold values from 0 to 1535, as said below
- cotangent: bfloat16 [8, 1536, 896], P('dp', 'ctx'), may hold values from -6 to 6
- attn_weight: bfloat16 [2048, 896], P(('dp', 'ctx'))
- gate_up: bfloat16 [9728, 896], P(('dp', 'ctx')), may hold values from -0.1875 to 0.1875
- down_weight: bfloat16 [4864, 896], P(('dp', 'ctx')), may hold values from -0.078125 to 0.078125
- gain_attn: bfloat16 [896], P('ctx'), may hold values from 0.25 to 1.75
- gain_mlp: bfloat16 [896], P('ctx'), may hold values from 0.25 to 1.75
- qkv_bias: bfloat16 [1152], P('ctx'), may hold values from -2 to 2
Outputs:
- layer_out: bfloat16 [8, 1536, 896], P('dp', 'ctx')
- input_grad: bfloat16 [8, 1536, 896], P('dp', 'ctx')
- attn_weight_grad: float32 [2048, 896], P(('dp', 'ctx'))
- gate_up_grad: float32 [9728, 896], P(('dp', 'ctx'))
- down_weight_grad: float32 [4864, 896], P(('dp', 'ctx'))
- gain_attn_grad: float32 [896], P('ctx')
- gain_mlp_grad: float32 [896], P('ctx')
- qkv_bias_grad: float32 [1152], P('ctx')
Inputs may be any that keep to these rules, and one draw needn't show every extreme that they name: doc_start never exceeds the token's own index, never falls along a sequence, and each token either starts its document or has its predecessor's doc_start. In every sequence one document begins among the first 384 tokens and ends among the last 384; the others hold 200 to 2000 tokens, fewer where the sequence's ends or that document cut them.
All inputs are finite; a program needn't handle non-finite values.
Results may differ from a plain program's by a relative error of at most 0.014.
Values may be sent and summed in bfloat16 or wider, within the bound.
A program may use at most 192 MiB of HBM per device.

v0:
```python
import math

import jax
import jax.numpy as jnp
from jax import lax
from jax.sharding import PartitionSpec as P

D = 896
HEADS = 14
KVH = 2
HD = 64
FF = 4864
KVD = 128
QKVD = 1152


epsilon = 1e-06
rope_base = 1000000.0
masked_value = -1e30


def rope_tables(positions):
    half_dim = HD // 2
    frequency = rope_base ** (-jnp.arange(half_dim).astype(jnp.float32) * (2.0 / HD))
    angles = positions.astype(jnp.float32)[:, None] * frequency[None, :]
    return (jnp.cos(angles)[:, None, :], jnp.sin(angles)[:, None, :])


def rotate(values, cosine, sine_part):
    half_dim = values.shape[-1] // 2
    first_half = values[..., :half_dim]
    second_half = values[..., half_dim:]
    return jnp.concatenate(
        [
            first_half * cosine - second_half * sine_part,
            second_half * cosine + first_half * sine_part,
        ],
        -1,
    )


def unrotate(grad_in, cosine, sine_part):
    half_dim = grad_in.shape[-1] // 2
    first_half = grad_in[..., :half_dim]
    second_half = grad_in[..., half_dim:]
    return jnp.concatenate(
        [
            first_half * cosine + second_half * sine_part,
            second_half * cosine - first_half * sine_part,
        ],
        -1,
    )


def norm_back(grad_out, values, factor, gain_vec):
    scaled = grad_out * gain_vec
    gain_grad = jnp.sum(grad_out * values * factor, 0)
    inner_mean = jnp.mean(scaled * values, -1, keepdims=True)
    return (gain_grad, factor * scaled - values * factor**3 * inner_mean)


def contract_rows(left_op, right_op):
    return lax.dot_general(
        left_op, right_op, (((0,), (0,)), ((), ())), preferred_element_type=jnp.float32
    )


def contract_cols(left_op, right_op):
    return lax.dot_general(
        left_op, right_op, (((1,), (1,)), ((), ())), preferred_element_type=jnp.float32
    )


def column_term(left_op, right_op):
    return contract_rows(left_op, right_op)


def block_scores(queries, key_block, block_idx, block_len, row_ids, doc_first):
    raw_scores = jnp.einsum(
        "qkgd,nkd->kgqn", queries, key_block, preferred_element_type=jnp.float32
    ) * HD ** (-0.5)
    columns = block_idx * block_len + jnp.arange(block_len, dtype=jnp.int32)
    allowed = (columns[None, :] <= row_ids[:, None]) & (columns[None, :] >= doc_first[:, None])
    return (jnp.where(allowed, raw_scores, masked_value), allowed)


def split_blocks(key_rows, value_rows):
    total_len = key_rows.shape[0]
    block_len = math.gcd(total_len, 1024)
    blocks = total_len // block_len
    key_tiles = key_rows.reshape(blocks, block_len, KVH, HD)
    value_tiles = value_rows.reshape(blocks, block_len, KVH, HD)
    indices = jnp.arange(blocks, dtype=jnp.int32)
    return (block_len, indices, key_tiles, value_tiles)


def attend_forward(queries, key_rows, value_rows, row_ids, doc_first):
    local_len, kv_heads, groups, head_dim = queries.shape
    block_len, indices, key_tiles, value_tiles = split_blocks(key_rows, value_rows)

    def first_pass(running, inputs):
        block_idx, key_block = inputs
        top_old, total_old = running
        masked, allowed = block_scores(queries, key_block, block_idx, block_len, row_ids, doc_first)
        top_new = jnp.maximum(top_old, jnp.max(masked, -1))
        exp_terms = jnp.where(allowed, jnp.exp(masked - top_new[..., None]), 0.0)
        return ((top_new, total_old * jnp.exp(top_old - top_new) + jnp.sum(exp_terms, -1)), None)

    start_top = jnp.full((kv_heads, groups, local_len), masked_value, jnp.float32)
    start_total = jnp.zeros((kv_heads, groups, local_len), jnp.float32)
    (row_top, row_total), _ = lax.scan(first_pass, (start_top, start_total), (indices, key_tiles))

    def second_pass(running, inputs):
        block_idx, key_block, value_block = inputs
        plain_sum, rest_sum = running
        masked, allowed = block_scores(queries, key_block, block_idx, block_len, row_ids, doc_first)
        prob_f = (
            jnp.where(allowed, jnp.exp(masked - row_top[..., None]), 0.0) / row_total[..., None]
        )
        prob_low = prob_f.astype(jnp.bfloat16)
        remainder = (prob_f - prob_low.astype(jnp.float32)).astype(jnp.bfloat16)
        plain_sum = plain_sum + jnp.einsum(
            "kgqn,nkd->qkgd", prob_low, value_block, preferred_element_type=jnp.float32
        )
        rest_sum = rest_sum + jnp.einsum(
            "kgqn,nkd->qkgd", remainder, value_block, preferred_element_type=jnp.float32
        )
        return ((plain_sum, rest_sum), None)

    zero_out = jnp.zeros((local_len, kv_heads, groups, head_dim), jnp.float32)
    (plain_sum, rest_sum), _ = lax.scan(
        second_pass, (zero_out, zero_out), (indices, key_tiles, value_tiles)
    )
    width = kv_heads * groups * head_dim
    return (
        row_top,
        row_total,
        plain_sum.reshape(local_len, width),
        (plain_sum + rest_sum).reshape(local_len, width),
    )


def attend_backward(
    queries, key_rows, value_rows, row_ids, doc_first, row_top, row_total, grad_out, row_delta
):
    local_len, kv_heads, groups, head_dim = queries.shape
    total_len = key_rows.shape[0]
    block_len, indices, key_tiles, value_tiles = split_blocks(key_rows, value_rows)
    scaling = HD ** (-0.5)

    def back_pass(running, inputs):
        block_idx, key_block, value_block = inputs
        masked, allowed = block_scores(queries, key_block, block_idx, block_len, row_ids, doc_first)
        prob_f = (
            jnp.where(allowed, jnp.exp(masked - row_top[..., None]), 0.0) / row_total[..., None]
        )
        prob_low = prob_f.astype(jnp.bfloat16)
        grad_prob = jnp.einsum(
            "qkgd,nkd->kgqn", grad_out, value_block, preferred_element_type=jnp.float32
        )
        grad_raw = (prob_f * (grad_prob - row_delta[..., None])).astype(jnp.bfloat16)
        new_q = (
            running
            + jnp.einsum("kgqn,nkd->qkgd", grad_raw, key_block, preferred_element_type=jnp.float32)
            * scaling
        )
        grad_k = (
            jnp.einsum("kgqn,qkgd->nkd", grad_raw, queries, preferred_element_type=jnp.float32)
            * scaling
        )
        grad_v = jnp.einsum(
            "kgqn,qkgd->nkd", prob_low, grad_out, preferred_element_type=jnp.float32
        )
        return (new_q, (grad_k, grad_v))

    zero_q = jnp.zeros((local_len, kv_heads, groups, head_dim), jnp.float32)
    grad_q, (grad_keys, grad_values) = lax.scan(
        back_pass, zero_q, (indices, key_tiles, value_tiles)
    )
    kv_width = kv_heads * head_dim
    grad_kv_rows = jnp.concatenate(
        [grad_keys.reshape(total_len, kv_width), grad_values.reshape(total_len, kv_width)], 1
    )
    return (grad_q.reshape(local_len, kv_heads * groups * head_dim), grad_kv_rows)


def on_device(
    hidden_in,
    doc_start,
    cotangent,
    attn_weight,
    gate_up,
    down_weight,
    gain_attn,
    gain_mlp,
    qkv_bias,
):
    stream = hidden_in[0].astype(jnp.float32)
    local_len = stream.shape[0]
    ctx_size = lax.axis_size("ctx")
    ctx_place = lax.axis_index("ctx")
    row_ids = ctx_place * local_len + jnp.arange(local_len, dtype=jnp.int32)
    doc_first = doc_start[0]
    cosine, sine_part = rope_tables(row_ids - doc_first)
    groups = HEADS // KVH
    weights = (
        lax.all_gather(attn_weight, ("dp", "ctx"), axis=0, tiled=True),
        lax.all_gather(gate_up, ("dp", "ctx"), axis=0, tiled=True),
        lax.all_gather(down_weight, ("dp", "ctx"), axis=0, tiled=True),
    )
    vectors = (
        lax.all_gather(gain_attn, "ctx", axis=0, tiled=True),
        lax.all_gather(gain_mlp, "ctx", axis=0, tiled=True),
        lax.all_gather(qkv_bias, "ctx", axis=0, tiled=True),
    )
    attn_full, gate_full, down_full = weights
    gain_one = vectors[0].astype(jnp.float32)
    gain_two = vectors[1].astype(jnp.float32)
    bias_full = vectors[2].astype(jnp.float32)
    factor_one = lax.rsqrt(jnp.mean(stream * stream, -1, keepdims=True) + epsilon)
    normed_one = (stream * factor_one * gain_one).astype(jnp.bfloat16)
    projected = contract_cols(normed_one, attn_full[:QKVD]) + bias_full
    queries = rotate(projected[:, :D].reshape(local_len, HEADS, HD), cosine, sine_part).astype(
        jnp.bfloat16
    )
    key_local = (
        rotate(projected[:, D : D + KVD].reshape(local_len, KVH, HD), cosine, sine_part)
        .astype(jnp.bfloat16)
        .reshape(local_len, KVD)
    )
    value_local = projected[:, D + KVD :].astype(jnp.bfloat16)
    key_rows, value_rows = (
        lax.all_gather(key_local, "ctx", axis=0, tiled=True),
        lax.all_gather(value_local, "ctx", axis=0, tiled=True),
    )
    grouped = queries.reshape(local_len, KVH, groups, HD)
    row_top, row_total, mixed_out, mixed_exact = attend_forward(
        grouped, key_rows, value_rows, row_ids, doc_first
    )
    mixed_low = mixed_out.astype(jnp.bfloat16)
    residual = stream + jnp.dot(mixed_low, attn_full[QKVD:], preferred_element_type=jnp.float32)
    factor_two = lax.rsqrt(jnp.mean(residual * residual, -1, keepdims=True) + epsilon)
    normed_two = (residual * factor_two * gain_two).astype(jnp.bfloat16)
    gate_up_act = contract_cols(normed_two, gate_full)
    gate_part = gate_up_act[:, :FF]
    up_part = gate_up_act[:, FF:]
    sigmoid_gate = jax.nn.sigmoid(gate_part)
    silu_gate = gate_part * sigmoid_gate
    activated = (silu_gate * up_part).astype(jnp.bfloat16)
    output = residual + jnp.dot(activated, down_full, preferred_element_type=jnp.float32)
    attn_back, gate_back, down_back = (
        lax.all_gather(attn_weight, ("dp", "ctx"), axis=0, tiled=True),
        lax.all_gather(gate_up, ("dp", "ctx"), axis=0, tiled=True),
        lax.all_gather(down_weight, ("dp", "ctx"), axis=0, tiled=True),
    )
    vectors_back = (
        lax.all_gather(gain_attn, "ctx", axis=0, tiled=True),
        lax.all_gather(gain_mlp, "ctx", axis=0, tiled=True),
        lax.all_gather(qkv_bias, "ctx", axis=0, tiled=True),
    )
    key_again, value_again = (
        lax.all_gather(key_local, "ctx", axis=0, tiled=True),
        lax.all_gather(value_local, "ctx", axis=0, tiled=True),
    )
    gain_one_back = vectors_back[0].astype(jnp.float32)
    gain_two_back = vectors_back[1].astype(jnp.float32)
    grad_two = cotangent[0]
    grad_stream = grad_two.astype(jnp.float32)
    grad_act = contract_cols(grad_two, down_back)
    grad_gate = grad_act * up_part * sigmoid_gate * (1.0 + gate_part * (1.0 - sigmoid_gate))
    grad_up = grad_act * silu_gate
    grad_gu = jnp.concatenate([grad_gate, grad_up], 1).astype(jnp.bfloat16)
    grad_normed = jnp.dot(grad_gu, gate_back, preferred_element_type=jnp.float32)
    gain_two_grad, grad_res = norm_back(grad_normed, residual, factor_two, gain_two_back)
    grad_mid = grad_stream + grad_res
    grad_mid_low = grad_mid.astype(jnp.bfloat16)
    grad_mixed = contract_cols(grad_mid_low, attn_back[QKVD:]).astype(jnp.bfloat16)
    grad_grouped = grad_mixed.reshape(local_len, KVH, groups, HD)
    exact_grouped = mixed_exact.reshape(local_len, KVH, groups, HD)
    row_delta = jnp.sum(grad_grouped.astype(jnp.float32) * exact_grouped, -1).transpose(1, 2, 0)
    grad_q, grad_kv_rows = attend_backward(
        grouped,
        key_again,
        value_again,
        row_ids,
        doc_first,
        row_top,
        row_total,
        grad_grouped,
        row_delta,
    )
    grad_kv = lax.psum_scatter(
        grad_kv_rows.astype(jnp.bfloat16), "ctx", scatter_dimension=0, tiled=True
    ).astype(jnp.float32)
    grad_q_raw = unrotate(grad_q.reshape(local_len, HEADS, HD), cosine, sine_part).reshape(
        local_len, D
    )
    grad_k_raw = unrotate(grad_kv[:, :KVD].reshape(local_len, KVH, HD), cosine, sine_part).reshape(
        local_len, KVD
    )
    grad_proj = jnp.concatenate([grad_q_raw, grad_k_raw, grad_kv[:, KVD:]], 1).astype(jnp.bfloat16)
    bias_grad = jnp.sum(grad_proj.astype(jnp.float32), 0)
    grad_normed_one = jnp.dot(grad_proj, attn_back[:QKVD], preferred_element_type=jnp.float32)
    gain_one_grad, grad_in = norm_back(grad_normed_one, stream, factor_one, gain_one_back)
    grad_input = grad_mid + grad_in
    proj_padded = jnp.concatenate([grad_proj, jnp.zeros((local_len, D), jnp.bfloat16)], 1)
    mixed_padded = jnp.concatenate([jnp.zeros((local_len, QKVD), jnp.bfloat16), mixed_low], 1)
    first_term = contract_rows(proj_padded, normed_one)
    second_term = contract_rows(mixed_padded, grad_mid_low)
    attn_sum = lax.psum_scatter(
        first_term + second_term, ("dp", "ctx"), scatter_dimension=0, tiled=True
    )
    gate_sum = lax.psum_scatter(
        column_term(grad_gu, normed_two), ("dp", "ctx"), scatter_dimension=0, tiled=True
    )
    down_sum = lax.psum_scatter(
        column_term(activated, grad_two), ("dp", "ctx"), scatter_dimension=0, tiled=True
    )
    vector_sums = lax.psum((gain_one_grad, gain_two_grad, bias_grad), ("dp", "ctx"))
    gain_len = D // ctx_size
    bias_len = QKVD // ctx_size
    gain_one_part = lax.dynamic_slice_in_dim(vector_sums[0], ctx_place * gain_len, gain_len)
    gain_two_part = lax.dynamic_slice_in_dim(vector_sums[1], ctx_place * gain_len, gain_len)
    bias_part = lax.dynamic_slice_in_dim(vector_sums[2], ctx_place * bias_len, bias_len)
    return (
        output.astype(jnp.bfloat16)[None],
        grad_input.astype(jnp.bfloat16)[None],
        attn_sum,
        gate_sum,
        down_sum,
        gain_one_part,
        gain_two_part,
        bias_part,
    )


def solution(mesh):
    in_specs = (
        P("dp", "ctx", None),
        P("dp", "ctx"),
        P("dp", "ctx", None),
        P(("dp", "ctx"), None),
        P(("dp", "ctx"), None),
        P(("dp", "ctx"), None),
        P("ctx"),
        P("ctx"),
        P("ctx"),
    )
    out_specs = (
        P("dp", "ctx", None),
        P("dp", "ctx", None),
        P(("dp", "ctx"), None),
        P(("dp", "ctx"), None),
        P(("dp", "ctx"), None),
        P("ctx"),
        P("ctx"),
        P("ctx"),
    )
    return jax.shard_map(
        on_device, mesh=mesh, in_specs=in_specs, out_specs=out_specs, check_vma=False
    )
```

profile of v0, /device:TPU:0, one launch (start us, length us, event | category | flops | bytes accessed | tf_op | source)
XLA Modules:
  0.0 1724.1 jit_solution(4928937906456728397)
XLA Ops:
  14.6 11.6 all-reduce.7
  29.7 44.3 %all-gather.4.cloned.1.call-done = bf16[2048,896]{1,0:T(8,128)(2,1)} async-done(((bf16[64,896]{1,0:T(8,128)(2,1)}), bf16[2048,896]{1,0:T(8,128)(2,1)}) %all-gather.4.cloned.1.call-update) | async-done | bytes 3670032 | tf_op jit(solution)/shard_map/all_gather | solution.py:207
  82.4 11.7 all_gather.35
  94.5 10.0 all_gather.34
  106.6 46.2 %while.41 = (s32[]{:T(128)}, f32[2,7,384]{2,1,0:T(8,128)}, f32[2,7,384]{2,1,0:T(8,128)}, s32[3]{0:T(128)S(1)}, s32[1,384]{1,0:T(1,128)S(1)}, /*index=5*/bf16[3,5...) while((s32[]{:T(128)}, f32[2,7,384]{2,1,0:T(8,128)}, ...), condition=%wide.region_4.5_spmd.clone, body=%wide.region_1.4_spmd.clone.sunk | while | flops 374959232 | bytes 23978740 | solution.py:111
  114.1 6.7 select_reduce_fusion.2
  128.9 6.7 select_reduce_fusion.2
  137.8 7.6 fusion.147
  145.4 6.8 select_reduce_fusion.2
  152.9 63.4 %while.42 = (s32[]{:T(128)}, f32[384,2,7,64]{0,3,2,1:T(8,128)S(1)}, f32[384,2,7,64]{0,3,2,1:T(8,128)}, bf16[3,512,2,64]{1,3,2,0:T(8,128)(2,1)S(1)}, s32[3]{0:T(1...) while((s32[]{:T(128)}, f32[384,2,7,64]{0,3,2,1:T(8,128)S(1)}, ...), condition=%wide.region_6.7_spmd.clone, body=%wide.region_5.6_spmd.clone.sunk | while | flops 1086456704 | bytes 84105080 | solution.py:131
  154.4 6.7 fusion.154
  161.1 10.0 select_add_fusion.2
  175.0 6.7 fusion.154
  181.7 10.8 select_add_fusion.2
  196.7 6.6 fusion.154
  203.4 10.5 select_add_fusion.2
  220.2 15.5 fusion.103
  235.7 39.2 %all-gather.8.cloned.1.call-done = bf16[4864,896]{1,0:T(8,128)(2,1)} async-done(((bf16[152,896]{1,0:T(8,128)(2,1)}), bf16[4864,896]{1,0:T(8,128)(2,1)}) %all-gather.8.cloned.1.call-update) | async-done | bytes 8716304 | tf_op jit(solution)/shard_map/all_gather | solution.py:209
  275.0 13.3 multiply_convert_fusion.1
  288.3 19.3 %multiply_reduce_fusion = (f32[896]{0:T(1024)}, f32[384]{0:T(512)S(1)}, f32[384,896]{1,0:T(8,128)S(1)}) fusion(f32[384,896]{1,0:T(8,128)S(1)} %copy-done.10, f32[384]{0:T(512)S(1)} %get-tuple-element.496, f32[896]{0:T(1024)S(1)} %copy-done.33, bf16[9728,896]{1,0:T(8,128)(2,1)} %all-gather.6.cloned.1.call-done, bf16[384,4864]{1,0:T(8,128)(2,1)} %get-tuple-element.479, ...), kind=kOutput, calls=%fused_computation.109 | convolution fusion | flops 6711114240 | bytes 27666432 | tf_op jit(solution)/shard_map/dot_general | solution.py:273
  316.0 81.2 %while.43 = (s32[]{:T(128)}, f32[384,2,7,64]{0,3,2,1:T(8,128)}, bf16[3,512,2,64]{1,3,2,0:T(8,128)(2,1)}, bf16[3,512,2,64]{1,3,2,0:T(8,128)(2,1)}, bf16[3,512,2,6...) while((s32[]{:T(128)}, f32[384,2,7,64]{0,3,2,1:T(8,128)}, ...), condition=%wide.region_11.12_spmd.clone, body=%wide.region_10.11_spmd.clone.sunk | while | flops 1788068736 | bytes 136743312 | solution.py:177
  336.5 6.6 fusion.170
  363.6 6.6 fusion.170
  390.7 6.6 fusion.170
  402.3 24.1 %reduce-scatter.14.cloned.1.call-done = bf16[384,256]{1,0:T(8,128)(2,1)} async-done(((bf16[1536,256]{1,0:T(8,128)(2,1)}), bf16[384,256]{1,0:T(8,128)(2,1)}) %reduce-scatter.14.cloned.1.call-update) | async-done | bytes 196624
  437.6 11.0 fusion.91
  450.0 20.1 %fusion.65 = f32[9728,896]{1,0:T(8,128)} fusion(bf16[384,4864]{1,0:T(8,128)(2,1)} %get-tuple-element.479, bf16[384,4864]{1,0:T(8,128)(2,1)} %copy-done.12, f32[384,896]{1,0:T(8,128)S(1)} %copy-done.11, f32[896]{0:T(1024)S(1)} %copy-done.34, f32[384]{0:T(512)S(1)} %copy-done.38), kind=kOutput, calls=%fused_computation.79 | convolution fusion | flops 6710083584 | bytes 43717632 | tf_op jit(solution)/shard_map/dot_general | solution.py:63
  470.1 9.7 fusion.89
  481.3 41.3 %all-reduce.6 = (f32[896]{0:T(1024)S(1)}, f32[896]{0:T(1024)S(1)}, f32[1152]{0:T(1024)S(1)}) all-reduce(f32[896]{0:T(1024)S(1)} %get-tuple-element.400, f32[896]{0:T(1024)S(1)} %copy-done.40, f32[1152]{0:T(1024)S(1)} %get-tuple-element.474), channel_id=1, replica_groups=mesh['dp'=8,'ctx'=4] {'dp','ctx'}, use_global_device_ids=true, to_apply=%region_18.19 | all-reduce | flops 2944 | bytes 23552 | tf_op jit(solution)/shard_map/psum | solution.py:319
  525.8 74.0 %reduce-scatter.10.cloned.1.call-done = f32[64,896]{1,0:T(8,128)} async-done(((f32[2048,896]{1,0:T(8,128)}), f32[64,896]{1,0:T(8,128)}) %reduce-scatter.10.cloned.1.call-update) | async-done | bytes 229392 | tf_op jit(solution)/shard_map/reduce_scatter | solution.py:310
  599.8 377.3 %reduce-scatter.16.cloned.1.call-done = f32[152,896]{1,0:T(8,128)} async-done(((f32[4864,896]{1,0:T(8,128)}), f32[152,896]{1,0:T(8,128)}) %reduce-scatter.16.cloned.1.call-update) | async-done | bytes 544784
  977.1 739.9 %reduce-scatter.12.cloned.1.call-done = f32[304,896]{1,0:T(8,128)} async-done(((f32[9728,896]{1,0:T(8,128)}), f32[304,896]{1,0:T(8,128)}) %reduce-scatter.12.cloned.1.call-update) | async-done | bytes 1089552 | tf_op jit(solution)/shard_map/reduce_scatter | solution.py:313
  (298 shorter events, 140.0 us)
Async XLA Ops:
  7.2 66.9 %all-gather.4.cloned.1.call-start = ((), (), s32[]{:S(2)}) async-start(), calls=%async_computation.4 | async-start | bytes 3784704 | tf_op jit(solution)/shard_map/all_gather | solution.py:207
  7.9 212.3 %all-gather.6.cloned.1.call-start = ((), (), s32[]{:S(2)}) async-start(), calls=%async_computation.5 | async-start | bytes 17977344 | tf_op jit(solution)/shard_map/all_gather | solution.py:208
  8.6 266.3 %all-gather.8.cloned.1.call-start = ((), (), s32[]{:S(2)}) async-start(), calls=%async_computation.6 | async-start | bytes 8988672 | tf_op jit(solution)/shard_map/all_gather | solution.py:209
  9.4 417.0 %reduce-scatter.14.cloned.1.call-start = ((), (), s32[]{:S(2)}) async-start(), calls=%async_computation.9 | async-start | bytes 983040
  26.2 50.9 %copy-start.31 = (f32[896]{0:T(1024)}, f32[896]{0:T(1024)S(1)}, u32[]{:S(2)}) copy-start(f32[896]{0:T(1024)S(1)} %convert_element_type.96) | copy-start | bytes 10756
  28.2 49.0 %copy-start.35 = (f32[384]{0:T(512)}, f32[384]{0:T(512)S(1)}, u32[]{:S(2)}) copy-start(f32[384]{0:T(512)S(1)} %get-tuple-element.494) | copy-start | bytes 4612
  29.7 52.7 %copy-start.21 = (f32[384,32]{0,1:T(8,128)}, f32[384,32]{0,1:T(8,128)S(1)}, u32[]{:S(2)}) copy-start(f32[384,32]{0,1:T(8,128)S(1)} %get-tuple-element.491) | copy-start | bytes 147460
  29.7 52.7 %copy-start.23 = (f32[384,32]{0,1:T(8,128)}, f32[384,32]{0,1:T(8,128)S(1)}, u32[]{:S(2)}) copy-start(f32[384,32]{0,1:T(8,128)S(1)} %get-tuple-element.492) | copy-start | bytes 147460
  94.4 12.2 copy-start.30
  114.1 6.8 copy-start.26
  137.8 7.6 copy-start.19
  145.4 6.8 copy-start.26
  152.9 63.5 %copy-start.8 = (bf16[1,384,896]{2,1,0:T(8,128)(2,1)S(1)}, bf16[1,384,896]{2,1,0:T(8,128)(2,1)}, u32[]{:S(2)}) copy-start(bf16[1,384,896]{2,1,0:T(8,128)(2,1)} %param.15) | copy-start | bytes 2064388
  161.1 11.0 copy-start.1
  181.7 12.2 copy-start.1
  203.4 11.6 copy-start.1
  220.2 87.4 %copy-start.37 = (f32[384]{0:T(512)}, f32[384]{0:T(512)S(1)}, u32[]{:S(2)}) copy-start(f32[384]{0:T(512)S(1)} %get-tuple-element.496) | copy-start | bytes 4612
  275.0 13.3 copy-start.10
  288.2 19.3 %copy-start.12 = (bf16[384,4864]{1,0:T(8,128)(2,1)}, bf16[384,4864]{1,0:T(8,128)(2,1)S(1)}, u32[]{:S(2)}) copy-start(bf16[384,4864]{1,0:T(8,128)(2,1)S(1)} %get-tuple-element.478) | copy-start | bytes 11206660
  288.3 19.3 %copy-start.15 = (bf16[1,384,896]{2,1,0:T(8,128)(2,1)S(1)}, bf16[1,384,896]{2,1,0:T(8,128)(2,1)}, u32[]{:S(2)}) copy-start(bf16[1,384,896]{2,1,0:T(8,128)(2,1)} %param.17) | copy-start | bytes 2064388
  317.5 8.2 copy-start.25
  344.6 8.2 copy-start.25
  371.7 8.2 copy-start.25
  401.5 198.4 %reduce-scatter.10.cloned.1.call-start = ((), (), s32[]{:S(2)}) async-start(), calls=%async_computation.7 | async-start | bytes 7569408 | tf_op jit(solution)/shard_map/reduce_scatter | solution.py:310
  402.2 26.7 %copy-start.9 = (bf16[1,384,896]{2,1,0:T(8,128)(2,1)S(1)}, bf16[1,384,896]{2,1,0:T(8,128)(2,1)}, u32[]{:S(2)}) copy-start(bf16[1,384,896]{2,1,0:T(8,128)(2,1)} %param.15) | copy-start | bytes 2064388
  402.2 26.7 %copy-start.32 = (f32[896]{0:T(1024)S(1)}, f32[896]{0:T(1024)}, u32[]{:S(2)}) copy-start(f32[896]{0:T(1024)} %copy-done.31) | copy-start | bytes 10756
  402.2 26.7 %copy-start.36 = (f32[384]{0:T(512)S(1)}, f32[384]{0:T(512)}, u32[]{:S(2)}) copy-start(f32[384]{0:T(512)} %copy-done.35) | copy-start | bytes 4612
  436.5 540.6 %reduce-scatter.16.cloned.1.call-start = ((), (), s32[]{:S(2)}) async-start(), calls=%async_computation.10 | async-start | bytes 17977344
  448.6 1268.4 %reduce-scatter.12.cloned.1.call-start = ((), (), s32[]{:S(2)}) async-start(), calls=%async_computation.8 | async-start | bytes 35954688 | tf_op jit(solution)/shard_map/reduce_scatter | solution.py:313
  470.1 9.7 copy-start.14
  470.1 9.7 copy-start.41
  479.9 44.7 %copy-start.39 = (f32[384]{0:T(512)S(1)}, f32[384]{0:T(512)}, u32[]{:S(2)}) copy-start(f32[384]{0:T(512)} %get-tuple-element.493) | copy-start | bytes 4612
  (46 other events, 120.9 us)
Sparse Core Ops, SparseCore 0:
  10.8 63.1 all-gather.3
  76.9 118.3 all-gather.5
  198.1 76.7 all-gather.7
  401.6 24.7 reduce-scatter.13
  436.6 163.1 reduce-scatter.9
  602.6 374.5 reduce-scatter.15
  980.0 736.9 reduce-scatter.11
where the time goes:
time: 1730 us; the launch traced here: 1720 us
  waiting for transfers between devices  1300 us (75%)
  matrix products  243 us (14%)
  blocking collectives  74.6 us (4%)
  local copies, waits for them, and re-layouts  48.7 us (3%)
  other arithmetic  32.9 us (2%)
    reduce_scatter x1, waiting for transfers between devices, on_device(): lax.psum_scatter(column_term(grad_gu, normed_two), ('dp', 'ctx'), scatter...  740 us
    unnamed x9, waiting for transfers between devices  403 us
    reduce_scatter x1, waiting for transfers between devices, on_device(): lax.psum_scatter(first_term + second_term, ('dp', 'ctx'), scatter_dimensi...  74 us
    dot_general x9, matrix products, block_scores(): jnp.einsum('qkgd,nkd->kgqn', queries, key_block, preferred_element_type=j...  51.3 us
    all_gather x1, waiting for transfers between devices, on_device(): lax.all_gather(attn_weight, ('dp', 'ctx'), axis=0, tiled=True)  44.3 us
    psum x1, blocking collectives, on_device(): lax.psum((gain_one_grad, gain_two_grad, bias_grad), ('dp', 'ctx'))  41.3 us
    all_gather x1, waiting for transfers between devices, on_device(): lax.all_gather(down_weight, ('dp', 'ctx'), axis=0, tiled=True)  39.2 us
    dot_general x4, matrix products, contract_rows(): lax.dot_general(left_op, right_op, (((0,), (0,)), ((), ())), preferred_el...  38.8 us
  transfers between devices with their start and end apart: 7, of which 6 were waited for; matrix products, arithmetic and copies ran while one was open for 11% of the time, Pallas kernels for 0%

commit v1 on v0

--- a/solution.py
+++ b/solution.py
@@ -73,6 +73,35 @@
 
 def column_term(left_op, right_op):
     return contract_rows(left_op, right_op)
+
+
+def index_bits(axis_name):
+    count = (lax.axis_size(axis_name) - 1).bit_length()
+    return [(axis_name, bit) for bit in reversed(range(count))]
+
+
+def split_bits(partial, bits):
+    rows = partial.shape[0] >> len(bits)
+    return partial.reshape([2] * len(bits) + [rows, partial.shape[1]])
+
+
+def halve(block, bits, step):
+    name, bit = step
+    place = bits.index(step)
+    mine = (lax.axis_index(name) >> bit) & 1
+    sent = lax.dynamic_index_in_dim(block, 1 - mine, place, keepdims=False)
+    kept = lax.dynamic_index_in_dim(block, mine, place, keepdims=False)
+    pairs = [(i, i ^ (1 << bit)) for i in range(lax.axis_size(name))]
+    got = lax.ppermute(sent, name, pairs)
+    total = kept.astype(jnp.float32) + got.astype(jnp.float32)
+    return (total, bits[:place] + bits[place + 1 :])
+
+
+def halve_all(block, bits, order):
+    total = block
+    for step in order:
+        total, bits = halve(total.astype(jnp.bfloat16), bits, step)
+    return total
 
 
 def block_scores(queries, key_block, block_idx, block_len, row_ids, doc_first):
@@ -208,15 +237,14 @@
         lax.all_gather(gate_up, ("dp", "ctx"), axis=0, tiled=True),
         lax.all_gather(down_weight, ("dp", "ctx"), axis=0, tiled=True),
     )
-    vectors = (
-        lax.all_gather(gain_attn, "ctx", axis=0, tiled=True),
-        lax.all_gather(gain_mlp, "ctx", axis=0, tiled=True),
-        lax.all_gather(qkv_bias, "ctx", axis=0, tiled=True),
-    )
+    gain_len = D // ctx_size
+    vectors = lax.all_gather(
+        jnp.concatenate([gain_attn, gain_mlp, qkv_bias]), "ctx", axis=0, tiled=False
+    ).astype(jnp.float32)
     attn_full, gate_full, down_full = weights
-    gain_one = vectors[0].astype(jnp.float32)
-    gain_two = vectors[1].astype(jnp.float32)
-    bias_full = vectors[2].astype(jnp.float32)
+    gain_one = vectors[:, :gain_len].reshape(-1)
+    gain_two = vectors[:, gain_len : 2 * gain_len].reshape(-1)
+    bias_full = vectors[:, 2 * gain_len :].reshape(-1)
     factor_one = lax.rsqrt(jnp.mean(stream * stream, -1, keepdims=True) + epsilon)
     normed_one = (stream * factor_one * gain_one).astype(jnp.bfloat16)
     projected = contract_cols(normed_one, attn_full[:QKVD]) + bias_full
@@ -229,10 +257,10 @@
         .reshape(local_len, KVD)
     )
     value_local = projected[:, D + KVD :].astype(jnp.bfloat16)
-    key_rows, value_rows = (
-        lax.all_gather(key_local, "ctx", axis=0, tiled=True),
-        lax.all_gather(value_local, "ctx", axis=0, tiled=True),
-    )
+    kv_rows = lax.all_gather(
+        jnp.concatenate([key_local, value_local], 1), "ctx", axis=0, tiled=True
+    )
+    key_rows, value_rows = kv_rows[:, :KVD], kv_rows[:, KVD:]
     grouped = queries.reshape(local_len, KVH, groups, HD)
     row_top, row_total, mixed_out, mixed_exact = attend_forward(
         grouped, key_rows, value_rows, row_ids, doc_first
@@ -248,40 +276,24 @@
     silu_gate = gate_part * sigmoid_gate
     activated = (silu_gate * up_part).astype(jnp.bfloat16)
     output = residual + jnp.dot(activated, down_full, preferred_element_type=jnp.float32)
-    attn_back, gate_back, down_back = (
-        lax.all_gather(attn_weight, ("dp", "ctx"), axis=0, tiled=True),
-        lax.all_gather(gate_up, ("dp", "ctx"), axis=0, tiled=True),
-        lax.all_gather(down_weight, ("dp", "ctx"), axis=0, tiled=True),
-    )
-    vectors_back = (
-        lax.all_gather(gain_attn, "ctx", axis=0, tiled=True),
-        lax.all_gather(gain_mlp, "ctx", axis=0, tiled=True),
-        lax.all_gather(qkv_bias, "ctx", axis=0, tiled=True),
-    )
-    key_again, value_again = (
-        lax.all_gather(key_local, "ctx", axis=0, tiled=True),
-        lax.all_gather(value_local, "ctx", axis=0, tiled=True),
-    )
-    gain_one_back = vectors_back[0].astype(jnp.float32)
-    gain_two_back = vectors_back[1].astype(jnp.float32)
     grad_two = cotangent[0]
     grad_stream = grad_two.astype(jnp.float32)
-    grad_act = contract_cols(grad_two, down_back)
+    grad_act = contract_cols(grad_two, down_full)
     grad_gate = grad_act * up_part * sigmoid_gate * (1.0 + gate_part * (1.0 - sigmoid_gate))
     grad_up = grad_act * silu_gate
     grad_gu = jnp.concatenate([grad_gate, grad_up], 1).astype(jnp.bfloat16)
-    grad_normed = jnp.dot(grad_gu, gate_back, preferred_element_type=jnp.float32)
-    gain_two_grad, grad_res = norm_back(grad_normed, residual, factor_two, gain_two_back)
+    grad_normed = jnp.dot(grad_gu, gate_full, preferred_element_type=jnp.float32)
+    gain_two_grad, grad_res = norm_back(grad_normed, residual, factor_two, gain_two)
     grad_mid = grad_stream + grad_res
     grad_mid_low = grad_mid.astype(jnp.bfloat16)
-    grad_mixed = contract_cols(grad_mid_low, attn_back[QKVD:]).astype(jnp.bfloat16)
+    grad_mixed = contract_cols(grad_mid_low, attn_full[QKVD:]).astype(jnp.bfloat16)
     grad_grouped = grad_mixed.reshape(local_len, KVH, groups, HD)
     exact_grouped = mixed_exact.reshape(local_len, KVH, groups, HD)
     row_delta = jnp.sum(grad_grouped.astype(jnp.float32) * exact_grouped, -1).transpose(1, 2, 0)
     grad_q, grad_kv_rows = attend_backward(
         grouped,
-        key_again,
-        value_again,
+        key_rows,
+        value_rows,
         row_ids,
         doc_first,
         row_top,
@@ -289,9 +301,8 @@
         grad_grouped,
         row_delta,
     )
-    grad_kv = lax.psum_scatter(
-        grad_kv_rows.astype(jnp.bfloat16), "ctx", scatter_dimension=0, tiled=True
-    ).astype(jnp.float32)
+    ctx_bits = index_bits("ctx")
+    grad_kv = halve_all(split_bits(grad_kv_rows, ctx_bits), ctx_bits, ctx_bits[::-1])
     grad_q_raw = unrotate(grad_q.reshape(local_len, HEADS, HD), cosine, sine_part).reshape(
         local_len, D
     )
@@ -300,24 +311,37 @@
     )
     grad_proj = jnp.concatenate([grad_q_raw, grad_k_raw, grad_kv[:, KVD:]], 1).astype(jnp.bfloat16)
     bias_grad = jnp.sum(grad_proj.astype(jnp.float32), 0)
-    grad_normed_one = jnp.dot(grad_proj, attn_back[:QKVD], preferred_element_type=jnp.float32)
-    gain_one_grad, grad_in = norm_back(grad_normed_one, stream, factor_one, gain_one_back)
+    grad_normed_one = jnp.dot(grad_proj, attn_full[:QKVD], preferred_element_type=jnp.float32)
+    gain_one_grad, grad_in = norm_back(grad_normed_one, stream, factor_one, gain_one)
     grad_input = grad_mid + grad_in
-    proj_padded = jnp.concatenate([grad_proj, jnp.zeros((local_len, D), jnp.bfloat16)], 1)
-    mixed_padded = jnp.concatenate([jnp.zeros((local_len, QKVD), jnp.bfloat16), mixed_low], 1)
-    first_term = contract_rows(proj_padded, normed_one)
-    second_term = contract_rows(mixed_padded, grad_mid_low)
-    attn_sum = lax.psum_scatter(
-        first_term + second_term, ("dp", "ctx"), scatter_dimension=0, tiled=True
-    )
-    gate_sum = lax.psum_scatter(
-        column_term(grad_gu, normed_two), ("dp", "ctx"), scatter_dimension=0, tiled=True
-    )
-    down_sum = lax.psum_scatter(
-        column_term(activated, grad_two), ("dp", "ctx"), scatter_dimension=0, tiled=True
-    )
-    vector_sums = lax.psum((gain_one_grad, gain_two_grad, bias_grad), ("dp", "ctx"))
-    gain_len = D // ctx_size
+    dp_bits = index_bits("dp")
+    all_bits = dp_bits + ctx_bits
+    core, chip_bits = dp_bits[-1], dp_bits[:-1][::-1]
+    ctx_up = ctx_bits[::-1]
+    down_term = column_term(activated, grad_two).astype(jnp.bfloat16)
+    down_sum = halve_all(
+        split_bits(down_term, all_bits), all_bits, [core] + chip_bits + ctx_up
+    )
+    gate_term = column_term(grad_gu, normed_two).astype(jnp.bfloat16)
+    gate_pair, pair_bits = halve(split_bits(gate_term, all_bits), all_bits, core)
+    cut = gate_pair.shape[-2] // 2
+    gate_pair = gate_pair.astype(jnp.bfloat16)
+    gate_sum = jnp.concatenate(
+        [
+            halve_all(gate_pair[..., :cut, :], pair_bits, ctx_up + chip_bits),
+            halve_all(gate_pair[..., cut:, :], pair_bits, ctx_bits + chip_bits),
+        ],
+        0,
+    )
+    attn_term = jnp.concatenate(
+        [contract_rows(grad_proj, normed_one), contract_rows(mixed_low, grad_mid_low)], 0
+    ).astype(jnp.bfloat16)
+    attn_sum = halve_all(
+        split_bits(attn_term, all_bits), all_bits, [core] + ctx_up + chip_bits
+    )
+    vector_terms = jnp.concatenate([gain_one_grad, gain_two_grad, bias_grad])
+    gathered = jnp.sum(lax.all_gather(vector_terms, ("dp", "ctx"), axis=0, tiled=False), 0)
+    vector_sums = (gathered[:D], gathered[D : 2 * D], gathered[2 * D :])
     bias_len = QKVD // ctx_size
     gain_one_part = lax.dynamic_slice_in_dim(vector_sums[0], ctx_place * gain_len, gain_len)
     gain_two_part = lax.dynamic_slice_in_dim(vector_sums[1], ctx_place * gain_len, gain_len)

time: 1730 us -> 742 us (0.43)
  waiting for transfers between devices: 1300 us -> 195 us
  blocking collectives: 74.6 us -> 134 us
  local copies, waits for them, and re-layouts: 48.7 us -> 83.6 us
  other arithmetic: 32.9 us -> 57.6 us
    reduce_scatter x2 -> x0, waiting for transfers between devices: 814 us -> none  [the longest x1 740 us: on_device(): lax.psum_scatter(column_term(grad_gu, normed_two), ('dp', 'ctx'), scatter...]
    unnamed x9 -> x3, waiting for transfers between devices: 403 us -> 2.06 us
    ppermute x0 -> x21, waiting for transfers between devices: none -> 102 us  [halve(): got = lax.ppermute(sent, name, pairs)]
    all_gather x2, blocking collectives: 21.7 us -> 123 us  [the longest x1 106 us: on_device(): lax.all_gather(vector_terms, ('dp', 'ctx'), axis=0, tiled=False)]
    psum x1 -> x0, blocking collectives: 41.3 us -> none  [on_device(): lax.psum((gain_one_grad, gain_two_grad, bias_grad), ('dp', 'ctx'))]
    dynamic_slice x0 -> x6, local copies, waits for them, and re-layouts: none -> 29.9 us  [the longest x3 18.4 us: halve(): kept = lax.dynamic_index_in_dim(block, mine, place, keepdims=False)]
    convert_element_type x3 -> x16, other arithmetic: 0.6 us -> 19.1 us  [the longest x15 13.9 us: halve_all(): total, bits = halve(total.astype(jnp.bfloat16), bits, step)]
  transfers between devices with their start and end apart: 7 -> 24, of which waited for: 6 -> 14; matrix products, arithmetic and copies ran while one was open for 11% -> 30% of each run, Pallas kernels for 0% -> 0%
where the time goes in v1:
time: 742 us; the launch traced here: 738 us
  matrix products  228 us (31%)
  waiting for transfers between devices  195 us (26%)
  blocking collectives  134 us (18%)
  local copies, waits for them, and re-layouts  83.6 us (11%)
  other arithmetic  57.6 us (8%)
  starting transfers between devices  17.3 us (2%)
  between operations  15.7 us (2%)
    all_gather x1, blocking collectives, on_device(): lax.all_gather(vector_terms, ('dp', 'ctx'), axis=0, tiled=False)  106 us
    ppermute x21, waiting for transfers between devices, halve(): got = lax.ppermute(sent, name, pairs)  102 us
    all_gather x1, waiting for transfers between devices, on_device(): lax.all_gather(attn_weight, ('dp', 'ctx'), axis=0, tiled=True)  46.3 us
    all_gather x1, waiting for transfers between devices, on_device(): lax.all_gather(down_weight, ('dp', 'ctx'), axis=0, tiled=True)  45.5 us
    dot_general x9, matrix products, block_scores(): jnp.einsum('qkgd,nkd->kgqn', queries, key_block, preferred_element_type=j...  45.1 us
    dot_general x4, matrix products, contract_cols(): lax.dot_general(left_op, right_op, (((1,), (1,)), ((), ())), preferred_el...  36.1 us
    dot_general x3, matrix products, second_pass(): jnp.einsum('kgqn,nkd->qkgd', remainder, value_block, preferred_element_ty...  30.9 us
    dot_general x4, matrix products, contract_rows(): lax.dot_general(left_op, right_op, (((0,), (0,)), ((), ())), preferred_el...  28.9 us
  transfers between devices with their start and end apart: 24, of which 14 were waited for; matrix products, arithmetic and copies ran while one was open for 30% of the time, Pallas kernels for 0%

profile of v1, /device:TPU:0, one launch (start us, length us, event | category | flops | bytes accessed | tf_op | source)
XLA Modules:
  0.0 738.3 jit_solution(13642023461553204645)
XLA Ops:
  12.3 11.5 %all-reduce = bf16[2944]{0:T(1024)(128)(2,1)S(1)} all-reduce(bf16[2944]{0:T(1024)(128)(2,1)S(1)} %dynamic-update-slice), channel_id=2, replica_groups=mesh['dp'=8,'ctx'=4] {'ctx'}, use_global_device_ids=true, to_apply=%add | all-reduce | flops 2944 | bytes 11776
  27.8 46.3 %all-gather.7.cloned.1.call-done = bf16[2048,896]{1,0:T(8,128)(2,1)} async-done(((bf16[64,896]{1,0:T(8,128)(2,1)}), bf16[2048,896]{1,0:T(8,128)(2,1)}) %all-gather.7.cloned.1.call-update) | async-done | bytes 3670032 | tf_op jit(solution)/shard_map/all_gather | solution.py:236
  77.7 16.4 %all_gather.27 = bf16[1536,256]{1,0:T(8,128)(2,1)S(1)} all-gather(bf16[384,256]{1,0:T(8,128)(2,1)S(1)} %pad_maximum_fusion.8), channel_id=1, replica_groups=mesh['dp'=8,'ctx'=4] {'ctx'}, dimensions={0}, use_global_device_ids=true | all-gather | bytes 983040 | tf_op jit(solution)/shard_map/all_gather | solution.py:260
  104.2 44.4 %while.41 = (s32[]{:T(128)}, f32[2,7,384]{2,1,0:T(8,128)S(1)}, f32[2,7,384]{2,1,0:T(8,128)S(1)}, s32[3]{0:T(128)S(1)}, s32[1,384]{1,0:T(1,128)S(1)}, /*index=5*/...) while((s32[]{:T(128)}, f32[2,7,384]{2,1,0:T(8,128)S(1)}, ...), condition=%wide.region_4.5_spmd.clone, body=%wide.region_1.4_spmd.clone.sunk | while | flops 374959232 | bytes 23720608 | solution.py:140
  111.6 6.8 select_reduce_fusion.2
  125.8 6.7 select_reduce_fusion.2
  140.2 8.3 %select_reduce_fusion.2 = f32[2,7,384]{2,1,0:T(8,128)S(1)} fusion(f32[2,512,384,7]{2,1,3,0:T(8,128)} %get-tuple-element.692, f32[2,7,384]{2,1,0:T(8,128)S(1)} %select_maximum_fusion.2, pred[384,512]{0,1:T(8,128)(4,1)S(1)} %compare_and_fusion.6), kind=kLoop, calls=%fused_computation.4.clone.1 | loop fusion | flops 13757184 | bytes 11249664 | tf_op jit(solution)/shard_map/while/body/eval_jaxpr/reduce_sum | solution.py:136
  148.6 60.5 %while.42 = (s32[]{:T(128)}, f32[384,2,7,64]{0,3,2,1:T(8,128)S(1)}, f32[384,2,7,64]{0,3,2,1:T(8,128)}, bf16[3,512,2,64]{1,3,2,0:T(8,128)(2,1)S(1)}, s32[3]{0:T(1...) while((s32[]{:T(128)}, f32[384,2,7,64]{0,3,2,1:T(8,128)S(1)}, ...), condition=%wide.region_6.7_spmd.clone, body=%wide.region_5.6_spmd.clone.sunk | while | flops 1086456704 | bytes 84111072 | solution.py:160
  156.0 10.0 %select_add_fusion.2 = f32[384,2,7,64]{0,3,2,1:T(8,128)} fusion(f32[384,2,7,64]{0,3,2,1:T(8,128)} %get-tuple-element.767, f32[2,7,384,512]{2,3,1,0:T(8,128)} %fusion.166, pred[]{:T(512)S(6)} %compare.10, bf16[3,512,2,64]{1,3,2,0:T(8,128)(2,1)S(1)} %get-tuple-element.782, s32[]{:T(128)} %get-tuple-element.765), kind=kOutput, calls=%fused_computation.29.clone.1 | convolution fusion | flops 364019712 | bytes 13893637 | tf_op jit(solution)/shard_map/while/body/eval_jaxpr/kgqn,nkd->qkgd/dot_general | solution.py:154
  175.8 10.5 %select_add_fusion.2 = f32[384,2,7,64]{0,3,2,1:T(8,128)} fusion(f32[384,2,7,64]{0,3,2,1:T(8,128)} %get-tuple-element.767, f32[2,7,384,512]{2,3,1,0:T(8,128)} %fusion.166, pred[]{:T(512)S(6)} %compare.10, bf16[3,512,2,64]{1,3,2,0:T(8,128)(2,1)S(1)} %get-tuple-element.782, s32[]{:T(128)} %get-tuple-element.765), kind=kOutput, calls=%fused_computation.29.clone.1 | convolution fusion | flops 364019712 | bytes 13893637 | tf_op jit(solution)/shard_map/while/body/eval_jaxpr/kgqn,nkd->qkgd/dot_general | solution.py:154
  196.2 10.3 %select_add_fusion.2 = f32[384,2,7,64]{0,3,2,1:T(8,128)} fusion(f32[384,2,7,64]{0,3,2,1:T(8,128)} %get-tuple-element.767, f32[2,7,384,512]{2,3,1,0:T(8,128)} %fusion.166, pred[]{:T(512)S(6)} %compare.10, bf16[3,512,2,64]{1,3,2,0:T(8,128)(2,1)S(1)} %get-tuple-element.782, s32[]{:T(128)} %get-tuple-element.765), kind=kOutput, calls=%fused_computation.29.clone.1 | convolution fusion | flops 364019712 | bytes 13893637 | tf_op jit(solution)/shard_map/while/body/eval_jaxpr/kgqn,nkd->qkgd/dot_general | solution.py:154
  213.3 15.5 %fusion.112 = f32[384,9728]{1,0:T(8,128)} fusion(bf16[9728,896]{1,0:T(8,128)(2,1)} %all-gather.9.cloned.1.call-done, f32[384,896]{1,0:T(8,128)} %get-tuple-element.510, f32[896]{0:T(1024)S(1)} %copy-done.32, f32[384]{0:T(512)S(1)} %get-tuple-element.508), kind=kOutput, calls=%fused_computation.224 | convolution fusion | flops 6695141376 | bytes 33756160 | tf_op jit(solution)/shard_map/dot_general | solution.py:69
  228.8 45.5 %all-gather.11.cloned.1.call-done = bf16[4864,896]{1,0:T(8,128)(2,1)} async-done(((bf16[152,896]{1,0:T(8,128)(2,1)}), bf16[4864,896]{1,0:T(8,128)(2,1)}) %all-gather.11.cloned.1.call-update) | async-done | bytes 8716304 | tf_op jit(solution)/shard_map/all_gather | solution.py:238
  274.3 14.2 %multiply_convert_fusion.1 = (bf16[384,4864]{1,0:T(8,128)(2,1)}, bf16[384,4864]{1,0:T(8,128)(2,1)}, bf16[384,4864]{1,0:T(8,128)(2,1)}) fusion(f32[384,9728]{1,0:T(8,128)} %fusion.112, bf16[4864,896]{1,0:T(8,128)(2,1)} %all-gather.11.cloned.1.call-done, bf16[1,384,896]{2,1,0:T(8,128)(2,1)S(1)} %copy-done.25), kind=kOutput, calls=%fused_computation.83 | convolution fusion | flops 3375071232 | bytes 35553280 | tf_op jit(solution)/shard_map/dot_general | solution.py:69
  288.6 16.5 %convolution_convert_fusion = bf16[9728,896]{1,0:T(8,128)(2,1)} fusion(bf16[384,4864]{1,0:T(8,128)(2,1)} %get-tuple-element.479, bf16[384,4864]{1,0:T(8,128)(2,1)} %get-tuple-element.478, f32[384,896]{1,0:T(8,128)} %get-tuple-element.510, f32[896]{0:T(1024)S(1)} %copy-done.32, f32[384]{0:T(512)S(1)} %get-tuple-element.508), kind=kOutput, calls=%fused_computation.73 | convolution fusion | flops 6718799872 | bytes 26285056 | tf_op jit(solution)/shard_map/dot_general | solution.py:63
  305.1 16.3 %multiply_reduce_fusion = (f32[896]{0:T(1024)}, f32[384]{0:T(512)S(1)}, f32[384,896]{1,0:T(8,128)S(1)}) fusion(f32[384,896]{1,0:T(8,128)} %get-tuple-element.510, f32[384]{0:T(512)S(1)} %get-tuple-element.508, f32[896]{0:T(1024)S(1)} %copy-done.32, bf16[9728,896]{1,0:T(8,128)(2,1)} %all-gather.9.cloned.1.call-done, ...), kind=kOutput, calls=%fused_computation.138 | convolution fusion | flops 6711114240 | bytes 27666432 | tf_op jit(solution)/shard_map/dot_general | solution.py:285
  329.3 81.5 %while.43 = (s32[]{:T(128)}, f32[384,2,7,64]{0,3,2,1:T(8,128)}, bf16[3,512,2,64]{1,3,2,0:T(8,128)(2,1)}, bf16[3,512,2,64]{1,3,2,0:T(8,128)(2,1)}, bf16[3,512,2,6...) while((s32[]{:T(128)}, f32[384,2,7,64]{0,3,2,1:T(8,128)}, ...), condition=%wide.region_11.12_spmd.clone, body=%wide.region_10.11_spmd.clone.sunk | while | flops 1788068736 | bytes 136660848 | solution.py:206
  349.9 6.6 fusion.182
  377.1 6.6 fusion.182
  404.3 6.5 fusion.182
  415.9 11.7 %constant_dynamic-slice_fusion.3 = (bf16[2,2,1,2,2,304,896]{6,5,4,3,2,1,0:T(8,128)(2,1)}, bf16[2,2,1,2,2,304,896]{6,5,4,3,2,1,0:T(8,128)(2,1)}) fusion(bf16[2,2,2,2,2,304,896]{6,5,4,3,2,1,0:T(8,128)(2,1)} %bitcast.342, s32[]{:T(128)S(6)} %select_n.108, s32[]{:T(128)S(6)} %select_n.109), kind=kLoop, calls=%fused_computation.210 | loop fusion | bytes 34865160 | tf_op jit(solution)/shard_map/jit(dynamic_index_in_dim)/dynamic_slice | solution.py:93
  427.6 7.7 %copy.124 = bf16[2,2,1,2,2,304,896]{6,5,0,1,4,3,2:T(8,128)(2,1)} copy(bf16[2,2,1,2,2,304,896]{6,5,4,3,2,1,0:T(8,128)(2,1)} %get-tuple-element.481) | data formatting | bytes 17432576 | tf_op jit(solution)/shard_map/jit(dynamic_index_in_dim)/dynamic_slice | solution.py:92
  435.4 9.9 %convolution_convert_fusion.1 = bf16[4864,896]{1,0:T(8,128)(2,1)} fusion(bf16[384,4864]{1,0:T(8,128)(2,1)} %get-tuple-element.482, bf16[1,384,896]{2,1,0:T(8,128)(2,1)S(1)} %copy-done.26), kind=kOutput, calls=%fused_computation.76 | convolution fusion | flops 3351412736 | bytes 13139968 | tf_op jit(solution)/shard_map/dot_general | solution.py:63
  447.8 6.2 collective-permute-done.1
  457.7 6.2 constant_dynamic-slice_fusion.1
  470.0 8.4 %fusion.95 = bf16[1,384,896]{2,1,0:T(8,128)(2,1)} fusion(f32[384,896]{1,0:T(8,128)S(1)} %copy-done.20, bf16[384,4864]{1,0:T(8,128)(2,1)S(1)} %copy-done.38, bf16[4864,896]{1,0:T(8,128)(2,1)} %all-gather.11.cloned.1.call-done), kind=kOutput, calls=%fused_computation.146 | convolution fusion | flops 3347742720 | bytes 14516224 | tf_op jit(solution)/shard_map/dot_general | solution.py:278
  481.2 10.3 %collective-permute-done.3 = bf16[2,2,2,64,896]{4,3,0,1,2:T(8,128)(2,1)S(1)} collective-permute-done((bf16[2,2,2,64,896]{4,3,0,1,2:T(8,128)(2,1)S(1)}, bf16[2,2,2,64,896]{4,3,0,1,2:T(8,128)(2,1)S(1)}, u32[]{:S(2)}, u32[]{:S(2)}) %collective-permute-start.3) | collective-permute-done | bytes 917536 | tf_op jit(solution)/shard_map/ppermute | solution.py:95
  513.3 106.4 %all-gather.2 = f32[32,1,2944]{2,1,0:T(1,128)S(1)} all-gather(f32[1,1,2944]{2,1,0:T(1,128)S(1)} %reshape.287), channel_id=3, replica_groups=mesh['dp'=8,'ctx'=4] {'dp','ctx'}, dimensions={0}, use_global_device_ids=true | all-gather | bytes 388608 | tf_op jit(solution)/shard_map/all_gather | solution.py:343
  641.5 30.9 %collective-permute-done.12 = bf16[2,2,2,152,896]{4,3,0,1,2:T(8,128)(2,1)S(1)} collective-permute-done((bf16[2,2,2,152,896]{4,3,0,1,2:T(8,128)(2,1)S(1)}, bf16[2,2,2,152,896]{4,3,0,1,2:T(8,128)(2,1)S(1)}, u32[]{:S(2)}, u32[]{:S(2)}) %collective-permute-start.12) | collective-permute-done | bytes 2179104 | tf_op jit(solution)/shard_map/ppermute | solution.py:95
  683.1 6.9 collective-permute-done.9
  700.4 7.6 %collective-permute-done.10 = bf16[2,152,896]{2,1,0:T(8,128)(2,1)S(1)} collective-permute-done((bf16[2,152,896]{2,1,0:T(8,128)(2,1)S(1)}, bf16[2,152,896]{2,1,0:T(8,128)(2,1)S(1)}, u32[]{:S(2)}, u32[]{:S(2)}) %collective-permute-start.10) | collective-permute-done | bytes 544800 | tf_op jit(solution)/shard_map/ppermute | solution.py:95
  715.8 10.8 %collective-permute-done.11 = bf16[152,896]{1,0:T(8,128)(2,1)S(1)} collective-permute-done((bf16[152,896]{1,0:T(8,128)(2,1)S(1)}, bf16[152,896]{1,0:T(8,128)(2,1)S(1)}, u32[]{:S(2)}, u32[]{:S(2)}) %collective-permute-start.11) | collective-permute-done | bytes 272416 | tf_op jit(solution)/shard_map/ppermute | solution.py:95
  (373 shorter events, 238.4 us)
Async XLA Ops:
  7.2 66.9 %all-gather.7.cloned.1.call-start = ((), (), s32[]{:S(2)}) async-start(), calls=%async_computation | async-start | bytes 3784704 | tf_op jit(solution)/shard_map/all_gather | solution.py:236
  7.9 205.3 %all-gather.9.cloned.1.call-start = ((), (), s32[]{:S(2)}) async-start(), calls=%async_computation.1 | async-start | bytes 17977344 | tf_op jit(solution)/shard_map/all_gather | solution.py:237
  8.6 265.7 %all-gather.11.cloned.1.call-start = ((), (), s32[]{:S(2)}) async-start(), calls=%async_computation.2 | async-start | bytes 8988672 | tf_op jit(solution)/shard_map/all_gather | solution.py:238
  24.1 53.0 %copy-start.30 = (f32[896]{0:T(1024)}, f32[896]{0:T(1024)S(1)}, u32[]{:S(2)}) copy-start(f32[896]{0:T(1024)S(1)} %mul.347) | copy-start | bytes 10756
  26.1 51.1 %copy-start.34 = (f32[384]{0:T(512)}, f32[384]{0:T(512)S(1)}, u32[]{:S(2)}) copy-start(f32[384]{0:T(512)S(1)} %get-tuple-element.506) | copy-start | bytes 4612
  27.8 49.6 %copy-start.21 = (f32[384,32]{0,1:T(8,128)}, f32[384,32]{0,1:T(8,128)S(1)}, u32[]{:S(2)}) copy-start(f32[384,32]{0,1:T(8,128)S(1)} %get-tuple-element.503) | copy-start | bytes 147460
  27.8 49.6 %copy-start.23 = (f32[384,32]{0,1:T(8,128)}, f32[384,32]{0,1:T(8,128)S(1)}, u32[]{:S(2)}) copy-start(f32[384,32]{0,1:T(8,128)S(1)} %get-tuple-element.504) | copy-start | bytes 147460
  213.3 61.1 %copy-start.25 = (bf16[1,384,896]{2,1,0:T(8,128)(2,1)S(1)}, bf16[1,384,896]{2,1,0:T(8,128)(2,1)}, u32[]{:S(2)}) copy-start(bf16[1,384,896]{2,1,0:T(8,128)(2,1)} %param.17) | copy-start | bytes 2064388
  414.6 31.8 %collective-permute-start = (bf16[2,384,256]{1,2,0:T(8,128)(2,1)S(1)}, bf16[2,384,256]{1,2,0:T(8,128)(2,1)S(1)}, u32[]{:S(2)}, u32[]{:S(2)}) collective-permute-start(bf16[2,384,256]{1,2,0:T(8,128)(2,1)S(1)} %dynamic-slice_bitcast_fusion.11), channel_id=1, source_target_pairs={{0,1},{1,0},{2,3},{3,2},{4,5},{5,4},{6,7},{7,6},{8,9},{9,8},{10,11... | collective-permute-start | bytes 1179656 | tf_op jit(solution)/shard_map/ppermute | solution.py:95
  435.4 64.2 %collective-permute-start.7 = (bf16[2,2,2,2,304,896]{5,4,0,1,3,2:T(8,128)(2,1)}, bf16[2,2,2,2,304,896]{5,4,0,1,3,2:T(8,128)(2,1)}, u32[]{:S(2)}, u32[]{:S(2)}) collective-permute-start(bf16[2,2,2,2,304,896]{5,4,0,1,3,2:T(8,128)(2,1)} %bitcast.352), channel_id=1, source_target_pairs={{0,4},{4,0},{8,12},{12,8},{16,20},{20,16},{24,28},{28,24},{1,5},{5... | collective-permute-start | bytes 26148872 | tf_op jit(solution)/shard_map/ppermute | solution.py:95
  446.6 7.4 collective-permute-start.1
  457.7 9.1 %collective-permute-start.2 = (bf16[2,2,2,2,64,896]{5,4,0,1,2,3:T(8,128)(2,1)}, bf16[2,2,2,2,64,896]{5,4,0,1,2,3:T(8,128)(2,1)}, u32[]{:S(2)}, u32[]{:S(2)}) collective-permute-start(bf16[2,2,2,2,64,896]{5,4,0,1,2,3:T(8,128)(2,1)} %bitcast.278), channel_id=1, source_target_pairs={{0,4},{4,0},{8,12},{12,8},{16,20},{20,16},{24,28},{28,24},{1,5},{5... | collective-permute-start | bytes 5505032 | tf_op jit(solution)/shard_map/ppermute | solution.py:95
  466.3 25.4 %collective-permute-start.16 = (bf16[2,2,2,2,152,896]{5,4,2,3,0,1:T(8,128)(2,1)}, bf16[2,2,2,2,152,896]{5,4,2,3,0,1:T(8,128)(2,1)}, u32[]{:S(2)}, u32[]{:S(2)}) collective-permute-start(bf16[2,2,2,2,152,896]{5,4,2,3,0,1:T(8,128)(2,1)} %bitcast.277), channel_id=1, source_target_pairs={{0,4},{4,0},{8,12},{12,8},{16,20},{20,16},{24,28},{28,24},{1,5},{5... | collective-permute-start | bytes 13074440 | tf_op jit(solution)/shard_map/ppermute | solution.py:95
  469.1 22.3 %collective-permute-start.3 = (bf16[2,2,2,64,896]{4,3,0,1,2:T(8,128)(2,1)S(1)}, bf16[2,2,2,64,896]{4,3,0,1,2:T(8,128)(2,1)S(1)}, u32[]{:S(2)}, u32[]{:S(2)}) collective-permute-start(bf16[2,2,2,64,896]{4,3,0,1,2:T(8,128)(2,1)S(1)} %dynamic-slice_bitcast_fusion.6), channel_id=1, source_target_pairs={{0,1},{1,0},{2,3},{3,2},{4,5},{5,4},{6,7},{7,6},{8,9},{9,8},{10,11... | collective-permute-start | bytes 2752520 | tf_op jit(solution)/shard_map/ppermute | solution.py:95
  498.1 132.9 %collective-permute-start.17 = (bf16[2,2,2,152,896]{4,3,1,2,0:T(8,128)(2,1)}, bf16[2,2,2,152,896]{4,3,1,2,0:T(8,128)(2,1)}, u32[]{:S(2)}, u32[]{:S(2)}) collective-permute-start(bf16[2,2,2,152,896]{4,3,1,2,0:T(8,128)(2,1)} %dynamic-slice_bitcast_fusion), channel_id=1, source_target_pairs={{0,8},{4,12},{8,0},{12,4},{16,24},{20,28},{24,16},{28,20},{1,9},{5... | collective-permute-start | bytes 6537224 | tf_op jit(solution)/shard_map/ppermute | solution.py:95
  507.6 123.4 %slice-start.5 = ((s8[4358144]{0:T(1024)(128)(4,1)}), s8[163840]{0:T(1024)(128)(4,1)S(1)}, s32[]{:S(2)}) async-start(s8[4358144]{0:T(1024)(128)(4,1)} %bitcast.345), calls=%async_computation.8 | async-start | bytes 327680
  510.3 126.0 %collective-permute-start.8 = (bf16[2,2,2,152,896]{4,3,0,1,2:T(8,128)(2,1)}, bf16[2,2,2,152,896]{4,3,0,1,2:T(8,128)(2,1)}, u32[]{:S(2)}, u32[]{:S(2)}) collective-permute-start(bf16[2,2,2,152,896]{4,3,0,1,2:T(8,128)(2,1)} %dynamic-slice_bitcast_fusion.2), channel_id=1, source_target_pairs={{0,1},{1,0},{2,3},{3,2},{4,5},{5,4},{6,7},{7,6},{8,9},{9,8},{10,11... | collective-permute-start | bytes 6537224 | tf_op jit(solution)/shard_map/ppermute | solution.py:95
  511.9 110.2 %collective-permute-start.4 = (bf16[2,2,64,896]{3,2,0,1:T(8,128)(2,1)}, bf16[2,2,64,896]{3,2,0,1:T(8,128)(2,1)}, u32[]{:S(2)}, u32[]{:S(2)}) collective-permute-start(bf16[2,2,64,896]{3,2,0,1:T(8,128)(2,1)} %dynamic-slice_bitcast_fusion.10), channel_id=1, source_target_pairs={{0,2},{1,3},{2,0},{3,1},{4,6},{5,7},{6,4},{7,5},{8,10},{9,11},{10,... | collective-permute-start | bytes 1376264 | tf_op jit(solution)/shard_map/ppermute | solution.py:95
  621.9 50.4 %collective-permute-start.12 = (bf16[2,2,2,152,896]{4,3,0,1,2:T(8,128)(2,1)S(1)}, bf16[2,2,2,152,896]{4,3,0,1,2:T(8,128)(2,1)S(1)}, u32[]{:S(2)}, u32[]{:S(2)}) collective-permute-start(bf16[2,2,2,152,896]{4,3,0,1,2:T(8,128)(2,1)S(1)} %dynamic-slice_bitcast_fusion.1), channel_id=1, source_target_pairs={{0,2},{1,3},{2,0},{3,1},{4,6},{5,7},{6,4},{7,5},{8,10},{9,11},{10,... | collective-permute-start | bytes 6537224 | tf_op jit(solution)/shard_map/ppermute | solution.py:95
  623.5 7.3 collective-permute-start.5
  630.9 44.1 %collective-permute-start.6 = (bf16[64,896]{1,0:T(8,128)(2,1)S(1)}, bf16[64,896]{1,0:T(8,128)(2,1)S(1)}, u32[]{:S(2)}, u32[]{:S(2)}) collective-permute-start(bf16[64,896]{1,0:T(8,128)(2,1)S(1)} %dynamic-slice_bitcast_fusion.17), channel_id=1, source_target_pairs={{0,16},{4,20},{8,24},{12,28},{16,0},{20,4},{24,8},{28,12},{1,17},{... | collective-permute-start | bytes 344072 | tf_op jit(solution)/shard_map/ppermute | solution.py:95
  633.3 39.0 %slice-start.7 = ((s8[4358144]{0:T(1024)(128)(4,1)}), s8[4194304]{0:T(1024)(128)(4,1)S(1)}, s32[]{:S(2)}) async-start(s8[4358144]{0:T(1024)(128)(4,1)} %bitcast.347), calls=%async_computation.10 | async-start | bytes 8388608
  633.5 38.9 %slice-start.8 = ((s8[4358144]{0:T(1024)(128)(4,1)}), s8[163840]{0:T(1024)(128)(4,1)S(1)}, s32[]{:S(2)}) async-start(s8[4358144]{0:T(1024)(128)(4,1)} %bitcast.347), calls=%async_computation.11 | async-start | bytes 327680
  633.5 46.7 %collective-permute-start.18 = (bf16[2,2,152,896]{3,2,0,1:T(8,128)(2,1)S(1)}, bf16[2,2,152,896]{3,2,0,1:T(8,128)(2,1)S(1)}, u32[]{:S(2)}, u32[]{:S(2)}) collective-permute-start(bf16[2,2,152,896]{3,2,0,1:T(8,128)(2,1)S(1)} %dynamic-slice_bitcast_fusion.3), channel_id=1, source_target_pairs={{0,16},{4,20},{8,24},{12,28},{16,0},{20,4},{24,8},{28,12},{1,17},{... | collective-permute-start | bytes 3268616 | tf_op jit(solution)/shard_map/ppermute | solution.py:95
  638.6 51.5 %collective-permute-start.9 = (bf16[2,2,152,896]{3,2,0,1:T(8,128)(2,1)S(1)}, bf16[2,2,152,896]{3,2,0,1:T(8,128)(2,1)S(1)}, u32[]{:S(2)}, u32[]{:S(2)}) collective-permute-start(bf16[2,2,152,896]{3,2,0,1:T(8,128)(2,1)S(1)} %dynamic-slice_bitcast_fusion.5), channel_id=1, source_target_pairs={{0,2},{1,3},{2,0},{3,1},{4,6},{5,7},{6,4},{7,5},{8,10},{9,11},{10,... | collective-permute-start | bytes 3268616 | tf_op jit(solution)/shard_map/ppermute | solution.py:95
  673.0 21.1 %collective-permute-start.13 = (bf16[2,2,152,896]{3,2,0,1:T(8,128)(2,1)S(1)}, bf16[2,2,152,896]{3,2,0,1:T(8,128)(2,1)S(1)}, u32[]{:S(2)}, u32[]{:S(2)}) collective-permute-start(bf16[2,2,152,896]{3,2,0,1:T(8,128)(2,1)S(1)} %dynamic-slice_bitcast_fusion.4), channel_id=1, source_target_pairs={{0,1},{1,0},{2,3},{3,2},{4,5},{5,4},{6,7},{7,6},{8,9},{9,8},{10,11... | collective-permute-start | bytes 3268616 | tf_op jit(solution)/shard_map/ppermute | solution.py:95
  680.5 19.5 %collective-permute-start.19 = (bf16[2,152,896]{2,1,0:T(8,128)(2,1)S(1)}, bf16[2,152,896]{2,1,0:T(8,128)(2,1)S(1)}, u32[]{:S(2)}, u32[]{:S(2)}) collective-permute-start(bf16[2,152,896]{2,1,0:T(8,128)(2,1)S(1)} %dynamic-slice_bitcast_fusion.7), channel_id=1, source_target_pairs={{0,1},{1,0},{2,3},{3,2},{4,5},{5,4},{6,7},{7,6},{8,9},{9,8},{10,11... | collective-permute-start | bytes 1634312 | tf_op jit(solution)/shard_map/ppermute | solution.py:95
  690.4 17.6 %collective-permute-start.10 = (bf16[2,152,896]{2,1,0:T(8,128)(2,1)S(1)}, bf16[2,152,896]{2,1,0:T(8,128)(2,1)S(1)}, u32[]{:S(2)}, u32[]{:S(2)}) collective-permute-start(bf16[2,152,896]{2,1,0:T(8,128)(2,1)S(1)} %dynamic-slice_bitcast_fusion.9), channel_id=1, source_target_pairs={{0,8},{4,12},{8,0},{12,4},{16,24},{20,28},{24,16},{28,20},{1,9},{5... | collective-permute-start | bytes 1634312 | tf_op jit(solution)/shard_map/ppermute | solution.py:95
  694.5 19.5 %collective-permute-start.14 = (bf16[2,152,896]{2,1,0:T(8,128)(2,1)S(1)}, bf16[2,152,896]{2,1,0:T(8,128)(2,1)S(1)}, u32[]{:S(2)}, u32[]{:S(2)}) collective-permute-start(bf16[2,152,896]{2,1,0:T(8,128)(2,1)S(1)} %dynamic-slice_bitcast_fusion.8), channel_id=1, source_target_pairs={{0,8},{4,12},{8,0},{12,4},{16,24},{20,28},{24,16},{28,20},{1,9},{5... | collective-permute-start | bytes 1634312 | tf_op jit(solution)/shard_map/ppermute | solution.py:95
  700.2 14.8 %collective-permute-start.20 = (bf16[152,896]{1,0:T(8,128)(2,1)S(1)}, bf16[152,896]{1,0:T(8,128)(2,1)S(1)}, u32[]{:S(2)}, u32[]{:S(2)}) collective-permute-start(bf16[152,896]{1,0:T(8,128)(2,1)S(1)} %dynamic-slice_bitcast_fusion.12), channel_id=1, source_target_pairs={{0,2},{1,3},{2,0},{3,1},{4,6},{5,7},{6,4},{7,5},{8,10},{9,11},{10,... | collective-permute-start | bytes 817160 | tf_op jit(solution)/shard_map/ppermute | solution.py:95
  708.2 18.3 %collective-permute-start.11 = (bf16[152,896]{1,0:T(8,128)(2,1)S(1)}, bf16[152,896]{1,0:T(8,128)(2,1)S(1)}, u32[]{:S(2)}, u32[]{:S(2)}) collective-permute-start(bf16[152,896]{1,0:T(8,128)(2,1)S(1)} %dynamic-slice_bitcast_fusion.14), channel_id=1, source_target_pairs={{0,16},{4,20},{8,24},{12,28},{16,0},{20,4},{24,8},{28,12},{1,17},{... | collective-permute-start | bytes 817160 | tf_op jit(solution)/shard_map/ppermute | solution.py:95
  714.1 16.4 %collective-permute-start.15 = (bf16[152,896]{1,0:T(8,128)(2,1)S(1)}, bf16[152,896]{1,0:T(8,128)(2,1)S(1)}, u32[]{:S(2)}, u32[]{:S(2)}) collective-permute-start(bf16[152,896]{1,0:T(8,128)(2,1)S(1)} %dynamic-slice_bitcast_fusion.13), channel_id=1, source_target_pairs={{0,16},{4,20},{8,24},{12,28},{16,0},{20,4},{24,8},{28,12},{1,17},{... | collective-permute-start | bytes 817160 | tf_op jit(solution)/shard_map/ppermute | solution.py:95
  (56 other events, 310.8 us)
Sparse Core Ops, SparseCore 0:
  10.8 63.1 all-gather.6
  76.9 117.7 all-gather.8
  197.5 76.7 all-gather.10

commit v2 on v1

v2 whole, which is shorter than its diff:
```python
import jax
import jax.numpy as jnp
from jax import lax
from jax.experimental import pallas as pl
from jax.experimental.pallas import tpu as pltpu
from jax.sharding import PartitionSpec as P

D = 896
HEADS = 14
KVH = 2
HD = 64
FF = 4864
KVD = 128
QKVD = 1152


epsilon = 1e-06
rope_base = 1000000.0
groups = HEADS // KVH
scaling = HD ** (-0.5)


def rope_tables(positions):
    half_dim = HD // 2
    frequency = rope_base ** (-jnp.arange(half_dim).astype(jnp.float32) * (2.0 / HD))
    angles = positions.astype(jnp.float32)[:, None] * frequency[None, :]
    return (jnp.cos(angles)[:, None, :], jnp.sin(angles)[:, None, :])


def rotate(values, cosine, sine_part):
    half_dim = values.shape[-1] // 2
    first_half = values[..., :half_dim]
    second_half = values[..., half_dim:]
    return jnp.concatenate(
        [
            first_half * cosine - second_half * sine_part,
            second_half * cosine + first_half * sine_part,
        ],
        -1,
    )


def unrotate(grad_in, cosine, sine_part):
    half_dim = grad_in.shape[-1] // 2
    first_half = grad_in[..., :half_dim]
    second_half = grad_in[..., half_dim:]
    return jnp.concatenate(
        [
            first_half * cosine + second_half * sine_part,
            second_half * cosine - first_half * sine_part,
        ],
        -1,
    )


def norm_back(grad_out, values, factor, gain_vec):
    scaled = grad_out * gain_vec
    gain_grad = jnp.sum(grad_out * values * factor, 0)
    inner_mean = jnp.mean(scaled * values, -1, keepdims=True)
    return (gain_grad, factor * scaled - values * factor**3 * inner_mean)


def contract_rows(left_op, right_op):
    return lax.dot_general(
        left_op, right_op, (((0,), (0,)), ((), ())), preferred_element_type=jnp.float32
    )


def contract_cols(left_op, right_op):
    return lax.dot_general(
        left_op, right_op, (((1,), (1,)), ((), ())), preferred_element_type=jnp.float32
    )


def column_term(left_op, right_op):
    return contract_rows(left_op, right_op)


def index_bits(axis_name):
    count = (lax.axis_size(axis_name) - 1).bit_length()
    return [(axis_name, bit) for bit in reversed(range(count))]


def split_bits(partial, bits):
    rows = partial.shape[0] >> len(bits)
    return partial.reshape([2] * len(bits) + [rows, partial.shape[1]])


def halve(block, bits, step):
    name, bit = step
    place = bits.index(step)
    mine = (lax.axis_index(name) >> bit) & 1
    sent = lax.dynamic_index_in_dim(block, 1 - mine, place, keepdims=False)
    kept = lax.dynamic_index_in_dim(block, mine, place, keepdims=False)
    pairs = [(i, i ^ (1 << bit)) for i in range(lax.axis_size(name))]
    got = lax.ppermute(sent, name, pairs)
    total = kept.astype(jnp.float32) + got.astype(jnp.float32)
    return (total, bits[:place] + bits[place + 1 :])


def halve_all(block, bits, order):
    total = block
    for step in order:
        total, bits = halve(total.astype(jnp.bfloat16), bits, step)
    return total


def partners(value, name):
    size = lax.axis_size(name)
    return [value] + [
        lax.ppermute(value, name, [(i, i ^ j) for i in range(size)]) for j in range(1, size)
    ]


def probabilities(keys, queries_t, cols, rows, first):
    scores = jnp.dot(keys, queries_t, preferred_element_type=jnp.float32) * scaling
    allowed = (cols <= rows) & (cols >= first)
    scores = jnp.where(allowed, scores, -jnp.inf)
    exp_terms = jnp.exp(scores - jnp.max(scores, 0, keepdims=True))
    return exp_terms * (1.0 / jnp.sum(exp_terms, 0, keepdims=True))


def forward_kernel(qt_ref, k_ref, vt_ref, col_ref, row_ref, first_ref, out_ref):
    prob = probabilities(k_ref[0], qt_ref[0], col_ref[...], row_ref[...], first_ref[...])
    out_ref[0] = jnp.dot(
        vt_ref[0], prob.astype(jnp.bfloat16), preferred_element_type=jnp.float32
    ).astype(jnp.bfloat16)


def backward_kernel(
    qt_ref, q_ref, gt_ref, g_ref, k_ref, kt_ref, v_ref, col_ref, row_ref, first_ref,
    dq_ref, dk_ref, dv_ref,
):
    @pl.when((pl.program_id(0) % groups == 0) & (pl.program_id(1) == 0))
    def _():
        dk_ref[...] = jnp.zeros_like(dk_ref)
        dv_ref[...] = jnp.zeros_like(dv_ref)

    prob = probabilities(k_ref[0], qt_ref[0], col_ref[...], row_ref[...], first_ref[...])
    grad_prob = jnp.dot(v_ref[0], gt_ref[0], preferred_element_type=jnp.float32)
    row_delta = jnp.sum(prob * grad_prob, 0, keepdims=True)
    grad_raw = (prob * (grad_prob - row_delta)).astype(jnp.bfloat16)
    dv_ref[0] += jnp.dot(prob.astype(jnp.bfloat16), g_ref[0], preferred_element_type=jnp.float32)
    dk_ref[0] += jnp.dot(grad_raw, q_ref[0], preferred_element_type=jnp.float32) * scaling
    dq_ref[0] = jnp.dot(kt_ref[0], grad_raw, preferred_element_type=jnp.float32) * scaling


def attention_specs(local_len, total_len):
    block = local_len if total_len <= 2048 or local_len % 128 else 128
    return (
        (HEADS, local_len // block),
        pl.BlockSpec((1, HD, block), lambda h, i: (h, 0, i)),
        pl.BlockSpec((1, block, HD), lambda h, i: (h, i, 0)),
        pl.BlockSpec((1, total_len, HD), lambda h, i: (h // groups, 0, 0)),
        pl.BlockSpec((1, HD, total_len), lambda h, i: (h // groups, 0, 0)),
        pl.BlockSpec((total_len, 1), lambda h, i: (0, 0)),
        pl.BlockSpec((1, block), lambda h, i: (0, i)),
    )


def attention_params(local_len, total_len, products):
    pairs = HEADS * local_len * total_len
    return dict(
        compiler_params=pltpu.CompilerParams(vmem_limit_bytes=48 * 1024 * 1024),
        cost_estimate=pl.CostEstimate(
            flops=2 * pairs * HD * products * 4, bytes_accessed=8 * 1024 * 1024, transcendentals=pairs
        ),
    )


def attend_forward(queries_t, keys, values_t, cols, rows, first):
    local_len, total_len = queries_t.shape[2], keys.shape[1]
    grid, wide, tall, key_rows, key_cols, col_spec, row_spec = attention_specs(local_len, total_len)
    return pl.pallas_call(
        forward_kernel,
        grid=grid,
        in_specs=[wide, key_rows, key_cols, col_spec, row_spec, row_spec],
        out_specs=wide,
        out_shape=jax.ShapeDtypeStruct((HEADS, HD, local_len), jnp.bfloat16),
        **attention_params(local_len, total_len, 2),
    )(queries_t, keys, values_t, cols, rows, first)


def attend_backward(queries_t, queries, grads_t, grads, keys, keys_t, values, cols, rows, first):
    local_len, total_len = queries_t.shape[2], keys.shape[1]
    grid, wide, tall, key_rows, key_cols, col_spec, row_spec = attention_specs(local_len, total_len)
    return pl.pallas_call(
        backward_kernel,
        grid=grid,
        in_specs=[wide, tall, wide, tall, key_rows, key_cols, key_rows]
        + [col_spec, row_spec, row_spec],
        out_specs=[wide, key_rows, key_rows],
        out_shape=[
            jax.ShapeDtypeStruct((HEADS, HD, local_len), jnp.float32),
            jax.ShapeDtypeStruct((KVH, total_len, HD), jnp.float32),
            jax.ShapeDtypeStruct((KVH, total_len, HD), jnp.float32),
        ],
        **attention_params(local_len, total_len, 5),
    )(queries_t, queries, grads_t, grads, keys, keys_t, values, cols, rows, first)


def on_device(
    hidden_in,
    doc_start,
    cotangent,
    attn_weight,
    gate_up,
    down_weight,
    gain_attn,
    gain_mlp,
    qkv_bias,
):
    stream = hidden_in[0].astype(jnp.float32)
    local_len = stream.shape[0]
    ctx_size = lax.axis_size("ctx")
    ctx_place = lax.axis_index("ctx")
    row_ids = ctx_place * local_len + jnp.arange(local_len, dtype=jnp.int32)
    doc_first = doc_start[0]
    cosine, sine_part = rope_tables(row_ids - doc_first)
    weights = (
        lax.all_gather(attn_weight, ("dp", "ctx"), axis=0, tiled=True),
        lax.all_gather(gate_up, ("dp", "ctx"), axis=0, tiled=True),
        lax.all_gather(down_weight, ("dp", "ctx"), axis=0, tiled=True),
    )
    gain_len = D // ctx_size
    places = jnp.arange(ctx_size, dtype=jnp.int32) ^ ctx_place
    vectors = jnp.stack(partners(jnp.concatenate([gain_attn, gain_mlp, qkv_bias]), "ctx"))
    vectors = jnp.take(vectors, places, axis=0).astype(jnp.float32)
    attn_full, gate_full, down_full = weights
    gain_one = vectors[:, :gain_len].reshape(-1)
    gain_two = vectors[:, gain_len : 2 * gain_len].reshape(-1)
    bias_full = vectors[:, 2 * gain_len :].reshape(-1)
    factor_one = lax.rsqrt(jnp.mean(stream * stream, -1, keepdims=True) + epsilon)
    normed_one = (stream * factor_one * gain_one).astype(jnp.bfloat16)
    projected = contract_cols(normed_one, attn_full[:QKVD]) + bias_full
    queries = rotate(projected[:, :D].reshape(local_len, HEADS, HD), cosine, sine_part).astype(
        jnp.bfloat16
    )
    key_local = (
        rotate(projected[:, D : D + KVD].reshape(local_len, KVH, HD), cosine, sine_part)
        .astype(jnp.bfloat16)
        .reshape(local_len, KVD)
    )
    value_local = projected[:, D + KVD :].astype(jnp.bfloat16)
    kv_rows = jnp.concatenate(
        partners(jnp.concatenate([key_local, value_local], 1), "ctx"), 0
    ).reshape(ctx_size * local_len, 2 * KVH, HD)
    kv_heads = kv_rows.transpose(1, 0, 2)
    kv_heads_t = kv_rows.transpose(1, 2, 0)
    cols = (places[:, None] * local_len + jnp.arange(local_len, dtype=jnp.int32)).reshape(-1, 1)
    place_args = (cols, row_ids[None, :], doc_first[None, :])
    queries_t = queries.transpose(1, 2, 0)
    mixed_t = attend_forward(queries_t, kv_heads[:KVH], kv_heads_t[KVH:], *place_args)
    mixed_low = mixed_t.transpose(2, 0, 1).reshape(local_len, D)
    residual = stream + jnp.dot(mixed_low, attn_full[QKVD:], preferred_element_type=jnp.float32)
    factor_two = lax.rsqrt(jnp.mean(residual * residual, -1, keepdims=True) + epsilon)
    normed_two = (residual * factor_two * gain_two).astype(jnp.bfloat16)
    gate_up_act = contract_cols(normed_two, gate_full)
    gate_part = gate_up_act[:, :FF]
    up_part = gate_up_act[:, FF:]
    sigmoid_gate = jax.nn.sigmoid(gate_part)
    silu_gate = gate_part * sigmoid_gate
    activated = (silu_gate * up_part).astype(jnp.bfloat16)
    output = residual + jnp.dot(activated, down_full, preferred_element_type=jnp.float32)
    grad_two = cotangent[0]
    grad_stream = grad_two.astype(jnp.float32)
    grad_act = contract_cols(grad_two, down_full)
    grad_gate = grad_act * up_part * sigmoid_gate * (1.0 + gate_part * (1.0 - sigmoid_gate))
    grad_up = grad_act * silu_gate
    grad_gu = jnp.concatenate([grad_gate, grad_up], 1).astype(jnp.bfloat16)
    grad_normed = jnp.dot(grad_gu, gate_full, preferred_element_type=jnp.float32)
    gain_two_grad, grad_res = norm_back(grad_normed, residual, factor_two, gain_two)
    grad_mid = grad_stream + grad_res
    grad_mid_low = grad_mid.astype(jnp.bfloat16)
    grad_mixed = contract_cols(grad_mid_low, attn_full[QKVD:]).astype(jnp.bfloat16)
    grad_heads = grad_mixed.reshape(local_len, HEADS, HD)
    grad_q_t, grad_keys, grad_values = attend_backward(
        queries_t,
        queries.transpose(1, 0, 2),
        grad_heads.transpose(1, 2, 0),
        grad_heads.transpose(1, 0, 2),
        kv_heads[:KVH],
        kv_heads_t[:KVH],
        kv_heads[KVH:],
        *place_args,
    )
    grad_q = grad_q_t.transpose(2, 0, 1)
    grad_kv_blocks = (
        jnp.concatenate([grad_keys, grad_values], 0)
        .astype(jnp.bfloat16)
        .reshape(2 * KVH, ctx_size, local_len, HD)
        .transpose(1, 2, 0, 3)
        .reshape(ctx_size, local_len, 2 * KVD)
    )
    grad_kv = grad_kv_blocks[0].astype(jnp.float32)
    for j in range(1, ctx_size):
        pairs = [(i, i ^ j) for i in range(ctx_size)]
        grad_kv = grad_kv + lax.ppermute(grad_kv_blocks[j], "ctx", pairs).astype(jnp.float32)
    ctx_bits = index_bits("ctx")
    grad_q_raw = unrotate(grad_q, cosine, sine_part).reshape(
        local_len, D
    )
    grad_k_raw = unrotate(grad_kv[:, :KVD].reshape(local_len, KVH, HD), cosine, sine_part).reshape(
        local_len, KVD
    )
    grad_proj = jnp.concatenate([grad_q_raw, grad_k_raw, grad_kv[:, KVD:]], 1).astype(jnp.bfloat16)
    bias_grad = jnp.sum(grad_proj.astype(jnp.float32), 0)
    grad_normed_one = jnp.dot(grad_proj, attn_full[:QKVD], preferred_element_type=jnp.float32)
    gain_one_grad, grad_in = norm_back(grad_normed_one, stream, factor_one, gain_one)
    grad_input = grad_mid + grad_in
    dp_bits = index_bits("dp")
    all_bits = dp_bits + ctx_bits
    core, chip_bits = dp_bits[-1], dp_bits[:-1][::-1]
    ctx_up = ctx_bits[::-1]
    down_term = column_term(activated, grad_two).astype(jnp.bfloat16)
    down_sum = halve_all(
        split_bits(down_term, all_bits), all_bits, [core] + chip_bits + ctx_up
    )
    gate_term = column_term(grad_gu, normed_two).astype(jnp.bfloat16)
    gate_pair, pair_bits = halve(split_bits(gate_term, all_bits), all_bits, core)
    cut = gate_pair.shape[-2] // 2
    gate_pair = gate_pair.astype(jnp.bfloat16)
    gate_sum = jnp.concatenate(
        [
            halve_all(gate_pair[..., :cut, :], pair_bits, ctx_up + chip_bits),
            halve_all(gate_pair[..., cut:, :], pair_bits, ctx_bits + chip_bits),
        ],
        0,
    )
    attn_term = jnp.concatenate(
        [contract_rows(grad_proj, normed_one), contract_rows(mixed_low, grad_mid_low)], 0
    ).astype(jnp.bfloat16)
    attn_sum = halve_all(
        split_bits(attn_term, all_bits), all_bits, [core] + ctx_up + chip_bits
    )
    bias_len = QKVD // ctx_size
    vector_sum = jnp.concatenate(
        [
            gain_one_grad.reshape(ctx_size, gain_len),
            gain_two_grad.reshape(ctx_size, gain_len),
            bias_grad.reshape(ctx_size, bias_len),
        ],
        1,
    ).reshape([2] * len(ctx_bits) + [2 * gain_len + bias_len])
    left = ctx_bits
    for step in ctx_up:
        vector_sum, left = halve(vector_sum, left, step)
    for name, bit in dp_bits[::-1]:
        pairs = [(i, i ^ (1 << bit)) for i in range(lax.axis_size(name))]
        vector_sum = vector_sum + lax.ppermute(vector_sum, name, pairs)
    gain_one_part = vector_sum[:gain_len]
    gain_two_part = vector_sum[gain_len : 2 * gain_len]
    bias_part = vector_sum[2 * gain_len :]
    return (
        output.astype(jnp.bfloat16)[None],
        grad_input.astype(jnp.bfloat16)[None],
        attn_sum,
        gate_sum,
        down_sum,
        gain_one_part,
        gain_two_part,
        bias_part,
    )


def solution(mesh):
    in_specs = (
        P("dp", "ctx", None),
        P("dp", "ctx"),
        P("dp", "ctx", None),
        P(("dp", "ctx"), None),
        P(("dp", "ctx"), None),
        P(("dp", "ctx"), None),
        P("ctx"),
        P("ctx"),
        P("ctx"),
    )
    out_specs = (
        P("dp", "ctx", None),
        P("dp", "ctx", None),
        P(("dp", "ctx"), None),
        P(("dp", "ctx"), None),
        P(("dp", "ctx"), None),
        P("ctx"),
        P("ctx"),
        P("ctx"),
    )
    return jax.shard_map(
        on_device, mesh=mesh, in_specs=in_specs, out_specs=out_specs, check_vma=False
    )
```

time: 742 us -> 644 us (0.87)
  blocking collectives: 134 us -> 0 us
  matrix products: 228 us -> 94.8 us
  waiting for transfers between devices: 195 us -> 327 us
  Pallas kernels: 0 us -> 61.6 us
  local copies, waits for them, and re-layouts: 83.6 us -> 65.8 us
  starting transfers between devices: 17.3 us -> 32 us
  other arithmetic: 57.6 us -> 43.9 us
    dot_general x27 -> x0, matrix products: 132 us -> none  [the longest x9 45.1 us: block_scores(): jnp.einsum('qkgd,nkd->kgqn', queries, key_block, preferred_element_type=j...]
    all_gather x2 -> x0, blocking collectives: 123 us -> none  [the longest x1 106 us: on_device(): lax.all_gather(vector_terms, ('dp', 'ctx'), axis=0, tiled=False)]
    all_gather x1, waiting for transfers between devices: 0.02 us -> 67.2 us  [on_device(): lax.all_gather(gate_up, ('dp', 'ctx'), axis=0, tiled=True)]
    pallas_call x0 -> x2, Pallas kernels: none -> 61.6 us  [the longest x1 39.9 us: attend_backward(): pl.pallas_call(backward_kernel, grid=grid, in_specs=[wide, tall, wide, ta...]
    ppermute x0 -> x12, waiting for transfers between devices: none -> 31.2 us  [the longest x3 31.2 us: on_device(): vector_sum = vector_sum + lax.ppermute(vector_sum, name, pairs)]
    reduce_sum x5 -> x0, other arithmetic: 23.7 us -> none  [the longest x3 21.8 us: first_pass(): jnp.sum(exp_terms, -1)]
    all_gather x1, waiting for transfers between devices: 45.5 us -> 64.9 us  [on_device(): lax.all_gather(down_weight, ('dp', 'ctx'), axis=0, tiled=True)]
    while x45 -> x0, local copies, waits for them, and re-layouts: 18.9 us -> none
  transfers between devices with their start and end apart: 24 -> 36, of which waited for: 14 -> 17; matrix products, arithmetic and copies ran while one was open for 30% -> 19% of each run, Pallas kernels for 0% -> 10%
where the time goes in v2:
time: 644 us; the launch traced here: 640 us
  waiting for transfers between devices  327 us (51%)
  matrix products  94.8 us (15%)
  local copies, waits for them, and re-layouts  65.8 us (10%)
  Pallas kernels  61.6 us (10%)
  other arithmetic  43.9 us (7%)
  starting transfers between devices  32 us (5%)
  between operations  15 us (2%)
    ppermute x21, waiting for transfers between devices, halve(): got = lax.ppermute(sent, name, pairs)  108 us
    all_gather x1, waiting for transfers between devices, on_device(): lax.all_gather(gate_up, ('dp', 'ctx'), axis=0, tiled=True)  67.2 us
    all_gather x1, waiting for transfers between devices, on_device(): lax.all_gather(down_weight, ('dp', 'ctx'), axis=0, tiled=True)  64.9 us
    all_gather x1, waiting for transfers between devices, on_device(): lax.all_gather(attn_weight, ('dp', 'ctx'), axis=0, tiled=True)  53.3 us
    pallas_call x1, Pallas kernels, attend_backward(): pl.pallas_call(backward_kernel, grid=grid, in_specs=[wide, tall, wide, ta...  39.9 us
    dot_general x4, matrix products, contract_cols(): lax.dot_general(left_op, right_op, (((1,), (1,)), ((), ())), preferred_el...  34.5 us
    ppermute x3, waiting for transfers between devices, on_device(): vector_sum = vector_sum + lax.ppermute(vector_sum, name, pairs)  31.2 us
    dot_general x4, matrix products, contract_rows(): lax.dot_general(left_op, right_op, (((0,), (0,)), ((), ())), preferred_el...  29.9 us
  transfers between devices with their start and end apart: 36, of which 17 were waited for; matrix products, arithmetic and copies ran while one was open for 19% of the time, Pallas kernels for 10%

profile of v2, /device:TPU:0, one launch (start us, length us, event | category | flops | bytes accessed | tf_op | source)
XLA Modules:
  0.0 640.0 jit_solution(9650400205099402320)
XLA Ops:
  10.2 2.9 collective-permute-start
  20.8 53.3 %all-gather.4.cloned.1.call-done = bf16[2048,896]{1,0:T(8,128)(2,1)} async-done(((bf16[64,896]{1,0:T(8,128)(2,1)}), bf16[2048,896]{1,0:T(8,128)(2,1)}) %all-gather.4.cloned.1.call-update) | async-done | bytes 3670032 | tf_op jit(solution)/shard_map/all_gather | solution.py:221
  88.0 3.0 copy.82
  104.1 21.7 %shard_map.152 = bf16[14,64,384]{2,1,0:T(8,128)(2,1)S(1)} custom-call(bf16[14,64,384]{2,1,0:T(8,128)(2,1)S(1)} %copy.63.qt_ref, bf16[2,1536,64]{2,1,0:T(8,128)(2,1)S(1)} %get-tuple-element.38.k_ref, bf16[2,64,1536]{2,1,0:T(8,128)(2,1)S(1)} %get-tuple-element.46.vt_ref, s32[1536,1]{1,0:T(8,128)S(1)} %bitcast.183, s32[1,384]{1,0:T(1,128)S(1)} %iota_add_fusion.row_ref, ...), custom_call_target="tpu_custom_call" | custom-call | flops 8455716864 | bytes 8388608 | tf_op jit(solution)/shard_map/pallas_call | solution.py:174
  129.0 67.2 %all-gather.6.cloned.1.call-done = bf16[9728,896]{1,0:T(8,128)(2,1)} async-done(((bf16[304,896]{1,0:T(8,128)(2,1)}), bf16[9728,896]{1,0:T(8,128)(2,1)}) %all-gather.6.cloned.1.call-update) | async-done | bytes 17432592 | tf_op jit(solution)/shard_map/all_gather | solution.py:222
  196.1 14.8 %fusion.55 = f32[384,9728]{1,0:T(8,128)} fusion(bf16[9728,896]{1,0:T(8,128)(2,1)} %all-gather.6.cloned.1.call-done, f32[384,896]{1,0:T(8,128)S(1)} %get-tuple-element.64, f32[896]{0:T(1024)S(1)} %mul.316, f32[384]{0:T(512)} %get-tuple-element.62), kind=kOutput, calls=%fused_computation.170 | convolution fusion | flops 6695141376 | bytes 33756160 | tf_op jit(solution)/shard_map/dot_general | solution.py:70
  210.9 64.9 %all-gather.8.cloned.1.call-done = bf16[4864,896]{1,0:T(8,128)(2,1)} async-done(((bf16[152,896]{1,0:T(8,128)(2,1)}), bf16[4864,896]{1,0:T(8,128)(2,1)}) %all-gather.8.cloned.1.call-update) | async-done | bytes 8716304 | tf_op jit(solution)/shard_map/all_gather | solution.py:223
  275.8 14.5 %multiply_convert_fusion.1 = (bf16[384,4864]{1,0:T(8,128)(2,1)}, bf16[384,4864]{1,0:T(8,128)(2,1)}, bf16[384,4864]{1,0:T(8,128)(2,1)}) fusion(f32[384,9728]{1,0:T(8,128)} %fusion.55, bf16[4864,896]{1,0:T(8,128)(2,1)} %all-gather.8.cloned.1.call-done, bf16[1,384,896]{2,1,0:T(8,128)(2,1)S(1)} %copy-done.28), kind=kOutput, calls=%fused_computation.11 | convolution fusion | flops 3375071232 | bytes 35553280 | tf_op jit(solution)/shard_map/dot_general | solution.py:70
  290.3 17.7 %convolution_convert_fusion = bf16[9728,896]{1,0:T(8,128)(2,1)} fusion(bf16[384,4864]{1,0:T(8,128)(2,1)} %get-tuple-element.21, bf16[384,4864]{1,0:T(8,128)(2,1)} %get-tuple-element.20, f32[384,896]{1,0:T(8,128)S(1)} %get-tuple-element.64, f32[896]{0:T(1024)S(1)} %mul.316, f32[384]{0:T(512)} %get-tuple-element.62), kind=kOutput, calls=%fused_computation.1 | convolution fusion | flops 6718799872 | bytes 26285056 | tf_op jit(solution)/shard_map/dot_general | solution.py:64
  308.0 16.0 %multiply_reduce_fusion = (f32[896]{0:T(1024)}, f32[384]{0:T(512)S(1)}, f32[384,896]{1,0:T(8,128)S(1)}) fusion(f32[384,896]{1,0:T(8,128)S(1)} %get-tuple-element.64, f32[384]{0:T(512)} %get-tuple-element.62, f32[896]{0:T(1024)S(1)} %mul.316, bf16[9728,896]{1,0:T(8,128)(2,1)} %all-gather.6.cloned.1.call-done, bf16[384,4864]{1,0:T(8,128)(2,1)} %get-tuple-element.21, ...), kind=kOutput, calls=%fused_computation.72 | convolution fusion | flops 6711114240 | bytes 27666432 | tf_op jit(solution)/shard_map/dot_general | solution.py:271
  329.9 11.8 %constant_dynamic-slice_fusion.7 = (bf16[2,2,1,2,2,304,896]{6,5,4,3,2,1,0:T(8,128)(2,1)}, bf16[2,2,1,2,2,304,896]{6,5,4,3,2,1,0:T(8,128)(2,1)}) fusion(bf16[2,2,2,2,2,304,896]{6,5,4,3,2,1,0:T(8,128)(2,1)} %bitcast.190, s32[]{:T(128)S(6)} %select_n.101, s32[]{:T(128)S(6)} %select_n.102), kind=kLoop, calls=%fused_computation.141 | loop fusion | bytes 34865160 | tf_op jit(solution)/shard_map/jit(dynamic_index_in_dim)/dynamic_slice | solution.py:94
  341.6 7.7 %copy.102 = bf16[2,2,1,2,2,304,896]{6,5,0,1,4,3,2:T(8,128)(2,1)} copy(bf16[2,2,1,2,2,304,896]{6,5,4,3,2,1,0:T(8,128)(2,1)} %get-tuple-element.23) | data formatting | bytes 17432576 | tf_op jit(solution)/shard_map/jit(dynamic_index_in_dim)/dynamic_slice | solution.py:93
  351.8 39.9 %shard_map.153 = (f32[14,64,384]{2,1,0:T(8,128)S(1)}, f32[2,1536,64]{2,1,0:T(8,128)}, f32[2,1536,64]{2,1,0:T(8,128)}) custom-call(bf16[14,64,384]{2,1,0:T(8,128)(2,1)S(1)} %copy-done.4, bf16[14,384,64]{2,1,0:T(8,128)(2,1)} %get-tuple-element.35.q_ref, bf16[14,64,384]{2,1,0:T(8,128)(2,1)S(1)} %bitcast.182, bf16[14,384,64]{2,1,0:T(8,128)(2,1)} %bitcast.203, ...), custom_call_target="tpu_custom_call" | custom-call | flops 21139292160 | bytes 8388608 | tf_op jit(solution)/shard_map/pallas_call | solution.py:187
  393.8 3.6 add_convert_fusion
  406.3 9.8 %convolution_convert_fusion.1 = bf16[4864,896]{1,0:T(8,128)(2,1)} fusion(bf16[384,4864]{1,0:T(8,128)(2,1)} %get-tuple-element.24, bf16[1,384,896]{2,1,0:T(8,128)(2,1)S(1)} %copy-done.29), kind=kOutput, calls=%fused_computation.4 | convolution fusion | flops 3351412736 | bytes 13139968 | tf_op jit(solution)/shard_map/dot_general | solution.py:64
  416.0 6.3 constant_dynamic-slice_fusion.5
  431.6 3.7 collective-permute-done.9
  441.7 4.0 fusion.27
  446.8 16.3 %collective-permute-done.28 = f32[2,736]{1,0:T(2,128)S(1)} collective-permute-done((f32[2,736]{1,0:T(2,128)S(1)}, f32[2,736]{1,0:T(2,128)S(1)}, u32[]{:S(2)}, u32[]{:S(2)}) %collective-permute-start.28) | collective-permute-done | bytes 5920 | tf_op jit(solution)/shard_map/ppermute | solution.py:96
  470.2 4.8 fusion.1
  476.8 5.2 fusion
  484.7 7.8 %fusion.31 = bf16[1,384,896]{2,1,0:T(8,128)(2,1)} fusion(f32[384,896]{1,0:T(8,128)S(1)} %copy-done.19, bf16[384,4864]{1,0:T(8,128)(2,1)S(1)} %copy-done.37, bf16[4864,896]{1,0:T(8,128)(2,1)} %all-gather.8.cloned.1.call-done), kind=kOutput, calls=%fused_computation.79 | convolution fusion | flops 3347742720 | bytes 14516224 | tf_op jit(solution)/shard_map/dot_general | solution.py:264
  494.3 30.6 %collective-permute-done.31 = f32[736]{0:T(1024)S(1)} collective-permute-done((f32[736]{0:T(1024)S(1)}, f32[736]{0:T(1024)S(1)}, u32[]{:S(2)}, u32[]{:S(2)}) %collective-permute-start.31) | collective-permute-done | bytes 2976 | tf_op jit(solution)/shard_map/ppermute | solution.py:350
  529.5 4.3 collective-permute-done.12
  540.6 3.5 collective-permute-done.19
  546.9 18.5 %collective-permute-done.13 = bf16[64,896]{1,0:T(8,128)(2,1)S(1)} collective-permute-done((bf16[64,896]{1,0:T(8,128)(2,1)S(1)}, bf16[64,896]{1,0:T(8,128)(2,1)S(1)}, u32[]{:S(2)}, u32[]{:S(2)}) %collective-permute-start.13) | collective-permute-done | bytes 114720 | tf_op jit(solution)/shard_map/ppermute | solution.py:96
  566.1 21.4 %collective-permute-done.25 = bf16[2,2,152,896]{3,2,0,1:T(8,128)(2,1)S(1)} collective-permute-done((bf16[2,2,152,896]{3,2,0,1:T(8,128)(2,1)S(1)}, bf16[2,2,152,896]{3,2,0,1:T(8,128)(2,1)S(1)}, u32[]{:S(2)}, u32[]{:S(2)}) %collective-permute-start.25) | collective-permute-done | bytes 1089568 | tf_op jit(solution)/shard_map/ppermute | solution.py:96
  591.3 9.8 %collective-permute-done.26 = bf16[2,152,896]{2,1,0:T(8,128)(2,1)S(1)} collective-permute-done((bf16[2,152,896]{2,1,0:T(8,128)(2,1)S(1)}, bf16[2,152,896]{2,1,0:T(8,128)(2,1)S(1)}, u32[]{:S(2)}, u32[]{:S(2)}) %collective-permute-start.26) | collective-permute-done | bytes 544800 | tf_op jit(solution)/shard_map/ppermute | solution.py:96
  601.9 5.2 collective-permute-done.17
  607.4 11.1 %collective-permute-done.21 = bf16[2,152,896]{2,1,0:T(8,128)(2,1)S(1)} collective-permute-done((bf16[2,152,896]{2,1,0:T(8,128)(2,1)S(1)}, bf16[2,152,896]{2,1,0:T(8,128)(2,1)S(1)}, u32[]{:S(2)}, u32[]{:S(2)}) %collective-permute-start.21) | collective-permute-done | bytes 544800 | tf_op jit(solution)/shard_map/ppermute | solution.py:96
  619.6 7.5 %collective-permute-done.18 = bf16[152,896]{1,0:T(8,128)(2,1)S(1)} collective-permute-done((bf16[152,896]{1,0:T(8,128)(2,1)S(1)}, bf16[152,896]{1,0:T(8,128)(2,1)S(1)}, u32[]{:S(2)}, u32[]{:S(2)}) %collective-permute-start.18) | collective-permute-done | bytes 272416 | tf_op jit(solution)/shard_map/ppermute | solution.py:96
  627.1 5.0 collective-permute-done.22
  (270 shorter events, 111.5 us)
Async XLA Ops:
  7.2 66.9 %all-gather.4.cloned.1.call-start = ((), (), s32[]{:S(2)}) async-start(), calls=%async_computation | async-start | bytes 3784704 | tf_op jit(solution)/shard_map/all_gather | solution.py:221
  7.9 188.2 %all-gather.6.cloned.1.call-start = ((), (), s32[]{:S(2)}) async-start(), calls=%async_computation.1 | async-start | bytes 17977344 | tf_op jit(solution)/shard_map/all_gather | solution.py:222
  8.7 267.1 %all-gather.8.cloned.1.call-start = ((), (), s32[]{:S(2)}) async-start(), calls=%async_computation.2 | async-start | bytes 8988672 | tf_op jit(solution)/shard_map/all_gather | solution.py:223
  10.2 9.5 %collective-permute-start = (bf16[736]{0:T(1024)(128)(2,1)S(1)}, bf16[736]{0:T(1024)(128)(2,1)S(1)}, u32[]{:S(2)}, u32[]{:S(2)}) collective-permute-start(bf16[736]{0:T(1024)(128)(2,1)S(1)} %pad_maximum_fusion.14), channel_id=1, source_target_pairs={{0,1},{1,0},{2,3},{3,2},{4,5},{5,4},{6,7},{7,6},{8,9},{9,8},{10,11... | collective-permute-start | bytes 4424 | tf_op jit(solution)/shard_map/ppermute | solution.py:111
  13.1 6.6 %collective-permute-start.1 = (bf16[736]{0:T(1024)(128)(2,1)S(1)}, bf16[736]{0:T(1024)(128)(2,1)S(1)}, u32[]{:S(2)}, u32[]{:S(2)}) collective-permute-start(bf16[736]{0:T(1024)(128)(2,1)S(1)} %pad_maximum_fusion.14), channel_id=1, source_target_pairs={{0,2},{1,3},{2,0},{3,1},{4,6},{5,7},{6,4},{7,5},{8,10},{9,11},{10,... | collective-permute-start | bytes 4424 | tf_op jit(solution)/shard_map/ppermute | solution.py:111
  79.2 17.0 %collective-permute-start.3 = (bf16[384,256]{1,0:T(8,128)(2,1)}, bf16[384,256]{1,0:T(8,128)(2,1)}, u32[]{:S(2)}, u32[]{:S(2)}) collective-permute-start(bf16[384,256]{1,0:T(8,128)(2,1)} %pad_maximum_fusion.9), channel_id=1, source_target_pairs={{0,1},{1,0},{2,3},{3,2},{4,5},{5,4},{6,7},{7,6},{8,9},{9,8},{10,11... | collective-permute-start | bytes 589832 | tf_op jit(solution)/shard_map/ppermute | solution.py:111
  80.7 15.6 %collective-permute-start.4 = (bf16[384,256]{1,0:T(8,128)(2,1)}, bf16[384,256]{1,0:T(8,128)(2,1)}, u32[]{:S(2)}, u32[]{:S(2)}) collective-permute-start(bf16[384,256]{1,0:T(8,128)(2,1)} %pad_maximum_fusion.9), channel_id=1, source_target_pairs={{0,2},{1,3},{2,0},{3,1},{4,6},{5,7},{6,4},{7,5},{8,10},{9,11},{10,... | collective-permute-start | bytes 589832 | tf_op jit(solution)/shard_map/ppermute | solution.py:111
  81.3 15.0 %collective-permute-start.5 = (bf16[384,256]{1,0:T(8,128)(2,1)}, bf16[384,256]{1,0:T(8,128)(2,1)}, u32[]{:S(2)}, u32[]{:S(2)}) collective-permute-start(bf16[384,256]{1,0:T(8,128)(2,1)} %pad_maximum_fusion.9), channel_id=1, source_target_pairs={{0,3},{1,2},{2,1},{3,0},{4,7},{5,6},{6,5},{7,4},{8,11},{9,10},{10,... | collective-permute-start | bytes 589832 | tf_op jit(solution)/shard_map/ppermute | solution.py:111
  349.4 127.3 %collective-permute-start.14 = (bf16[2,2,2,2,304,896]{5,4,0,1,3,2:T(8,128)(2,1)}, bf16[2,2,2,2,304,896]{5,4,0,1,3,2:T(8,128)(2,1)}, u32[]{:S(2)}, u32[]{:S(2)}) collective-permute-start(bf16[2,2,2,2,304,896]{5,4,0,1,3,2:T(8,128)(2,1)} %bitcast.192), channel_id=1, source_target_pairs={{0,4},{4,0},{8,12},{12,8},{16,20},{20,16},{24,28},{28,24},{1,5},{5... | collective-permute-start | bytes 26148872 | tf_op jit(solution)/shard_map/ppermute | solution.py:96
  402.7 23.2 %collective-permute-start.6 = (bf16[384,256]{0,1:T(8,128)(2,1)S(1)}, bf16[384,256]{0,1:T(8,128)(2,1)S(1)}, u32[]{:S(2)}, u32[]{:S(2)}) collective-permute-start(bf16[384,256]{0,1:T(8,128)(2,1)S(1)} %bitcast.212), channel_id=1, source_target_pairs={{0,1},{1,0},{2,3},{3,2},{4,5},{5,4},{6,7},{7,6},{8,9},{9,8},{10,11... | collective-permute-start | bytes 589832 | tf_op jit(solution)/shard_map/ppermute | solution.py:298
  404.0 21.9 %collective-permute-start.7 = (bf16[384,256]{0,1:T(8,128)(2,1)S(1)}, bf16[384,256]{0,1:T(8,128)(2,1)S(1)}, u32[]{:S(2)}, u32[]{:S(2)}) collective-permute-start(bf16[384,256]{0,1:T(8,128)(2,1)S(1)} %bitcast.211), channel_id=1, source_target_pairs={{0,2},{1,3},{2,0},{3,1},{4,6},{5,7},{6,4},{7,5},{8,10},{9,11},{10,... | collective-permute-start | bytes 589832 | tf_op jit(solution)/shard_map/ppermute | solution.py:298
  404.8 21.1 %collective-permute-start.8 = (bf16[384,256]{0,1:T(8,128)(2,1)S(1)}, bf16[384,256]{0,1:T(8,128)(2,1)S(1)}, u32[]{:S(2)}, u32[]{:S(2)}) collective-permute-start(bf16[384,256]{0,1:T(8,128)(2,1)S(1)} %bitcast.210), channel_id=1, source_target_pairs={{0,3},{1,2},{2,1},{3,0},{4,7},{5,6},{6,5},{7,4},{8,11},{9,10},{10,... | collective-permute-start | bytes 589832 | tf_op jit(solution)/shard_map/ppermute | solution.py:298
  424.7 45.4 %collective-permute-start.23 = (bf16[2,2,2,2,152,896]{5,4,2,3,0,1:T(8,128)(2,1)}, bf16[2,2,2,2,152,896]{5,4,2,3,0,1:T(8,128)(2,1)}, u32[]{:S(2)}, u32[]{:S(2)}) collective-permute-start(bf16[2,2,2,2,152,896]{5,4,2,3,0,1:T(8,128)(2,1)} %bitcast.178), channel_id=1, source_target_pairs={{0,4},{4,0},{8,12},{12,8},{16,20},{20,16},{24,28},{28,24},{1,5},{5... | collective-permute-start | bytes 13074440 | tf_op jit(solution)/shard_map/ppermute | solution.py:96
  440.1 26.7 %collective-permute-start.10 = (bf16[2,2,2,64,896]{4,3,0,1,2:T(8,128)(2,1)}, bf16[2,2,2,64,896]{4,3,0,1,2:T(8,128)(2,1)}, u32[]{:S(2)}, u32[]{:S(2)}) collective-permute-start(bf16[2,2,2,64,896]{4,3,0,1,2:T(8,128)(2,1)} %dynamic-slice_bitcast_fusion.6), channel_id=1, source_target_pairs={{0,1},{1,0},{2,3},{3,2},{4,5},{5,4},{6,7},{7,6},{8,9},{9,8},{10,11... | collective-permute-start | bytes 2752520 | tf_op jit(solution)/shard_map/ppermute | solution.py:96
  445.9 17.2 %collective-permute-start.28 = (f32[2,736]{1,0:T(2,128)S(1)}, f32[2,736]{1,0:T(2,128)S(1)}, u32[]{:S(2)}, u32[]{:S(2)}) collective-permute-start(f32[2,736]{1,0:T(2,128)S(1)} %bitcast.214), channel_id=1, source_target_pairs={{0,1},{1,0},{2,3},{3,2},{4,5},{5,4},{6,7},{7,6},{8,9},{9,8},{10,11... | collective-permute-start | bytes 17672 | tf_op jit(solution)/shard_map/ppermute | solution.py:96
  466.8 25.7 %collective-permute-start.30 = (f32[736]{0:T(1024)S(1)}, f32[736]{0:T(1024)S(1)}, u32[]{:S(2)}, u32[]{:S(2)}) collective-permute-start(f32[736]{0:T(1024)S(1)} %add.343), channel_id=1, source_target_pairs={{0,4},{4,0},{8,12},{12,8},{16,20},{20,16},{24,28},{28,24},{1,5},{5... | collective-permute-start | bytes 8840 | tf_op jit(solution)/shard_map/ppermute | solution.py:350
  468.6 58.2 %collective-permute-start.11 = (bf16[2,2,64,896]{3,2,0,1:T(8,128)(2,1)S(1)}, bf16[2,2,64,896]{3,2,0,1:T(8,128)(2,1)S(1)}, u32[]{:S(2)}, u32[]{:S(2)}) collective-permute-start(bf16[2,2,64,896]{3,2,0,1:T(8,128)(2,1)S(1)} %dynamic-slice_bitcast_fusion.10), channel_id=1, source_target_pairs={{0,2},{1,3},{2,0},{3,1},{4,6},{5,7},{6,4},{7,5},{8,10},{9,11},{10,... | collective-permute-start | bytes 1376264 | tf_op jit(solution)/shard_map/ppermute | solution.py:96
  475.2 59.8 %collective-permute-start.24 = (bf16[2,2,2,152,896]{4,3,1,2,0:T(8,128)(2,1)S(1)}, bf16[2,2,2,152,896]{4,3,1,2,0:T(8,128)(2,1)}, u32[]{:S(2)}, u32[]{:S(2)}) collective-permute-start(bf16[2,2,2,152,896]{4,3,1,2,0:T(8,128)(2,1)S(1)} %dynamic-slice_bitcast_fusion), channel_id=1, source_target_pairs={{0,8},{4,12},{8,0},{12,4},{16,24},{20,28},{24,16},{28,20},{1,9},{5... | collective-permute-start | bytes 6537224 | tf_op jit(solution)/shard_map/ppermute | solution.py:96
  483.4 55.9 %collective-permute-start.15 = (bf16[2,2,2,152,896]{4,3,0,1,2:T(8,128)(2,1)S(1)}, bf16[2,2,2,152,896]{4,3,0,1,2:T(8,128)(2,1)S(1)}, u32[]{:S(2)}, u32[]{:S(2)}) collective-permute-start(bf16[2,2,2,152,896]{4,3,0,1,2:T(8,128)(2,1)S(1)} %dynamic-slice_bitcast_fusion.2), channel_id=1, source_target_pairs={{0,1},{1,0},{2,3},{3,2},{4,5},{5,4},{6,7},{7,6},{8,9},{9,8},{10,11... | collective-permute-start | bytes 6537224 | tf_op jit(solution)/shard_map/ppermute | solution.py:96
  492.5 32.3 %collective-permute-start.31 = (f32[736]{0:T(1024)S(1)}, f32[736]{0:T(1024)S(1)}, u32[]{:S(2)}, u32[]{:S(2)}) collective-permute-start(f32[736]{0:T(1024)S(1)} %add.344), channel_id=1, source_target_pairs={{0,8},{4,12},{8,0},{12,4},{16,24},{20,28},{24,16},{28,20},{1,9},{5... | collective-permute-start | bytes 8840 | tf_op jit(solution)/shard_map/ppermute | solution.py:350
  493.7 50.3 %collective-permute-start.19 = (bf16[2,2,2,152,896]{4,3,0,1,2:T(8,128)(2,1)S(1)}, bf16[2,2,2,152,896]{4,3,0,1,2:T(8,128)(2,1)S(1)}, u32[]{:S(2)}, u32[]{:S(2)}) collective-permute-start(bf16[2,2,2,152,896]{4,3,0,1,2:T(8,128)(2,1)S(1)} %dynamic-slice_bitcast_fusion.1), channel_id=1, source_target_pairs={{0,2},{1,3},{2,0},{3,1},{4,6},{5,7},{6,4},{7,5},{8,10},{9,11},{10,... | collective-permute-start | bytes 6537224 | tf_op jit(solution)/shard_map/ppermute | solution.py:96
  527.0 6.8 %collective-permute-start.12 = (bf16[2,64,896]{2,1,0:T(8,128)(2,1)S(1)}, bf16[2,64,896]{2,1,0:T(8,128)(2,1)S(1)}, u32[]{:S(2)}, u32[]{:S(2)}) collective-permute-start(bf16[2,64,896]{2,1,0:T(8,128)(2,1)S(1)} %dynamic-slice_bitcast_fusion.14), channel_id=1, source_target_pairs={{0,8},{4,12},{8,0},{12,4},{16,24},{20,28},{24,16},{28,20},{1,9},{5... | collective-permute-start | bytes 688136 | tf_op jit(solution)/shard_map/ppermute | solution.py:96
  533.9 31.5 %collective-permute-start.13 = (bf16[64,896]{1,0:T(8,128)(2,1)S(1)}, bf16[64,896]{1,0:T(8,128)(2,1)S(1)}, u32[]{:S(2)}, u32[]{:S(2)}) collective-permute-start(bf16[64,896]{1,0:T(8,128)(2,1)S(1)} %dynamic-slice_bitcast_fusion.15), channel_id=1, source_target_pairs={{0,16},{4,20},{8,24},{12,28},{16,0},{20,4},{24,8},{28,12},{1,17},{... | collective-permute-start | bytes 344072 | tf_op jit(solution)/shard_map/ppermute | solution.py:96
  537.3 50.3 %collective-permute-start.25 = (bf16[2,2,152,896]{3,2,0,1:T(8,128)(2,1)S(1)}, bf16[2,2,152,896]{3,2,0,1:T(8,128)(2,1)S(1)}, u32[]{:S(2)}, u32[]{:S(2)}) collective-permute-start(bf16[2,2,152,896]{3,2,0,1:T(8,128)(2,1)S(1)} %dynamic-slice_bitcast_fusion.3), channel_id=1, source_target_pairs={{0,16},{4,20},{8,24},{12,28},{16,0},{20,4},{24,8},{28,12},{1,17},{... | collective-permute-start | bytes 3268616 | tf_op jit(solution)/shard_map/ppermute | solution.py:96
  539.9 48.5 %collective-permute-start.16 = (bf16[2,2,152,896]{3,2,0,1:T(8,128)(2,1)S(1)}, bf16[2,2,152,896]{3,2,0,1:T(8,128)(2,1)S(1)}, u32[]{:S(2)}, u32[]{:S(2)}) collective-permute-start(bf16[2,2,152,896]{3,2,0,1:T(8,128)(2,1)S(1)} %dynamic-slice_bitcast_fusion.5), channel_id=1, source_target_pairs={{0,2},{1,3},{2,0},{3,1},{4,6},{5,7},{6,4},{7,5},{8,10},{9,11},{10,... | collective-permute-start | bytes 3268616 | tf_op jit(solution)/shard_map/ppermute | solution.py:96
  544.8 44.1 %collective-permute-start.20 = (bf16[2,2,152,896]{3,2,0,1:T(8,128)(2,1)S(1)}, bf16[2,2,152,896]{3,2,0,1:T(8,128)(2,1)S(1)}, u32[]{:S(2)}, u32[]{:S(2)}) collective-permute-start(bf16[2,2,152,896]{3,2,0,1:T(8,128)(2,1)S(1)} %dynamic-slice_bitcast_fusion.4), channel_id=1, source_target_pairs={{0,1},{1,0},{2,3},{3,2},{4,5},{5,4},{6,7},{7,6},{8,9},{9,8},{10,11... | collective-permute-start | bytes 3268616 | tf_op jit(solution)/shard_map/ppermute | solution.py:96
  587.9 13.3 %collective-permute-start.26 = (bf16[2,152,896]{2,1,0:T(8,128)(2,1)S(1)}, bf16[2,152,896]{2,1,0:T(8,128)(2,1)S(1)}, u32[]{:S(2)}, u32[]{:S(2)}) collective-permute-start(bf16[2,152,896]{2,1,0:T(8,128)(2,1)S(1)} %dynamic-slice_bitcast_fusion.7), channel_id=1, source_target_pairs={{0,1},{1,0},{2,3},{3,2},{4,5},{5,4},{6,7},{7,6},{8,9},{9,8},{10,11... | collective-permute-start | bytes 1634312 | tf_op jit(solution)/shard_map/ppermute | solution.py:96
  588.8 18.3 %collective-permute-start.17 = (bf16[2,152,896]{2,1,0:T(8,128)(2,1)S(1)}, bf16[2,152,896]{2,1,0:T(8,128)(2,1)S(1)}, u32[]{:S(2)}, u32[]{:S(2)}) collective-permute-start(bf16[2,152,896]{2,1,0:T(8,128)(2,1)S(1)} %dynamic-slice_bitcast_fusion.9), channel_id=1, source_target_pairs={{0,8},{4,12},{8,0},{12,4},{16,24},{20,28},{24,16},{28,20},{1,9},{5... | collective-permute-start | bytes 1634312 | tf_op jit(solution)/shard_map/ppermute | solution.py:96
  589.2 29.2 %collective-permute-start.21 = (bf16[2,152,896]{2,1,0:T(8,128)(2,1)S(1)}, bf16[2,152,896]{2,1,0:T(8,128)(2,1)S(1)}, u32[]{:S(2)}, u32[]{:S(2)}) collective-permute-start(bf16[2,152,896]{2,1,0:T(8,128)(2,1)S(1)} %dynamic-slice_bitcast_fusion.8), channel_id=1, source_target_pairs={{0,8},{4,12},{8,0},{12,4},{16,24},{20,28},{24,16},{28,20},{1,9},{5... | collective-permute-start | bytes 1634312 | tf_op jit(solution)/shard_map/ppermute | solution.py:96
  601.3 17.4 %collective-permute-start.27 = (bf16[152,896]{1,0:T(8,128)(2,1)S(1)}, bf16[152,896]{1,0:T(8,128)(2,1)S(1)}, u32[]{:S(2)}, u32[]{:S(2)}) collective-permute-start(bf16[152,896]{1,0:T(8,128)(2,1)S(1)} %dynamic-slice_bitcast_fusion.11), channel_id=1, source_target_pairs={{0,2},{1,3},{2,0},{3,1},{4,6},{5,7},{6,4},{7,5},{8,10},{9,11},{10,... | collective-permute-start | bytes 817160 | tf_op jit(solution)/shard_map/ppermute | solution.py:96
  607.3 19.8 %collective-permute-start.18 = (bf16[152,896]{1,0:T(8,128)(2,1)S(1)}, bf16[152,896]{1,0:T(8,128)(2,1)S(1)}, u32[]{:S(2)}, u32[]{:S(2)}) collective-permute-start(bf16[152,896]{1,0:T(8,128)(2,1)S(1)} %dynamic-slice_bitcast_fusion.13), channel_id=1, source_target_pairs={{0,16},{4,20},{8,24},{12,28},{16,0},{20,4},{24,8},{28,12},{1,17},{... | collective-permute-start | bytes 817160 | tf_op jit(solution)/shard_map/ppermute | solution.py:96
  618.7 13.5 %collective-permute-start.22 = (bf16[152,896]{1,0:T(8,128)(2,1)S(1)}, bf16[152,896]{1,0:T(8,128)(2,1)S(1)}, u32[]{:S(2)}, u32[]{:S(2)}) collective-permute-start(bf16[152,896]{1,0:T(8,128)(2,1)S(1)} %dynamic-slice_bitcast_fusion.12), channel_id=1, source_target_pairs={{0,16},{4,20},{8,24},{12,28},{16,0},{20,4},{24,8},{28,12},{1,17},{... | collective-permute-start | bytes 817160 | tf_op jit(solution)/shard_map/ppermute | solution.py:96
  (45 other events, 815.1 us)
Sparse Core Ops, SparseCore 0:
  10.9 63.1 all-gather.3
  76.9 119.1 all-gather.5
  198.9 76.8 all-gather.7

commit v3 on v2

--- a/solution.py
+++ b/solution.py
@@ -18,6 +18,30 @@
 rope_base = 1000000.0
 groups = HEADS // KVH
 scaling = HD ** (-0.5)
+
+
+def double(block, held, step, all_bits):
+    name, bit = step
+    pairs = [(i, i ^ (1 << bit)) for i in range(lax.axis_size(name))]
+    got = lax.ppermute(block, name, pairs)
+    held = [other for other in all_bits if other in held or other == step]
+    is_low = (lax.axis_index(name) >> bit) & 1 == 0
+    low, high = jnp.where(is_low, block, got), jnp.where(is_low, got, block)
+    return (jnp.stack([low, high], held.index(step)), held)
+
+
+def gather_halves(shard):
+    dp_bits, ctx_bits = index_bits("dp"), index_bits("ctx")
+    all_bits = dp_bits + ctx_bits
+    cut = shard.shape[0] // 2
+    halves = []
+    for part, ctx_order in ((shard[:cut], ctx_bits), (shard[cut:], ctx_bits[::-1])):
+        held = []
+        for step in dp_bits[:-1] + ctx_order:
+            part, held = double(part, held, step, all_bits)
+        halves.append(part)
+    full, held = double(jnp.concatenate(halves, -2), held, dp_bits[-1], all_bits)
+    return full.reshape(-1, shard.shape[1])
 
 
 def rope_tables(positions):
@@ -219,7 +243,7 @@
     cosine, sine_part = rope_tables(row_ids - doc_first)
     weights = (
         lax.all_gather(attn_weight, ("dp", "ctx"), axis=0, tiled=True),
-        lax.all_gather(gate_up, ("dp", "ctx"), axis=0, tiled=True),
+        gather_halves(gate_up),
         lax.all_gather(down_weight, ("dp", "ctx"), axis=0, tiled=True),
     )
     gain_len = D // ctx_size

time: 644 us -> 628 us (0.975)
  waiting for transfers between devices: 327 us -> 252 us
  other arithmetic: 43.9 us -> 78 us
  starting transfers between devices: 32 us -> 52.9 us
    ppermute x0 -> x9, waiting for transfers between devices: none -> 114 us  [double(): got = lax.ppermute(block, name, pairs)]
    all_gather x1 -> x0, waiting for transfers between devices: 67.2 us -> none  [on_device(): lax.all_gather(gate_up, ('dp', 'ctx'), axis=0, tiled=True)]
    all_gather x1, waiting for transfers between devices: 64.9 us -> 0.01 us  [on_device(): lax.all_gather(down_weight, ('dp', 'ctx'), axis=0, tiled=True)]
    all_gather x1, waiting for transfers between devices: 53.3 us -> 0.01 us  [on_device(): lax.all_gather(attn_weight, ('dp', 'ctx'), axis=0, tiled=True)]
    another operation x6 -> x22, other arithmetic: 9.35 us -> 40.5 us  [the longest x16 31 us: double(): return (jnp.stack([low, high], held.index(step)), held)]
    ppermute x0 -> x9, starting transfers between devices: none -> 14.7 us  [double(): got = lax.ppermute(block, name, pairs)]
    unnamed x87 -> x127, local copies, waits for them, and re-layouts: 12.6 us -> 16.3 us
  transfers between devices with their start and end apart: 36 -> 44, of which waited for: 17 -> 20; matrix products, arithmetic and copies ran while one was open for 19% -> 25% of each run, Pallas kernels for 10% -> 10%
where the time goes in v3:
time: 628 us; the launch traced here: 623 us
  waiting for transfers between devices  252 us (40%)
  matrix products  93 us (15%)
  other arithmetic  78 us (12%)
  local copies, waits for them, and re-layouts  70.7 us (11%)
  Pallas kernels  61.3 us (10%)
  starting transfers between devices  52.9 us (8%)
  between operations  15.6 us (2%)
    ppermute x9, waiting for transfers between devices, double(): got = lax.ppermute(block, name, pairs)  114 us
    ppermute x21, waiting for transfers between devices, halve(): got = lax.ppermute(sent, name, pairs)  107 us
    pallas_call x1, Pallas kernels, attend_backward(): pl.pallas_call(backward_kernel, grid=grid, in_specs=[wide, tall, wide, ta...  39.7 us
    dot_general x4, matrix products, contract_cols(): lax.dot_general(left_op, right_op, (((1,), (1,)), ((), ())), preferred_el...  34.1 us
    another operation x16, other arithmetic, double(): return (jnp.stack([low, high], held.index(step)), held)  31 us
    ppermute x3, waiting for transfers between devices, on_device(): vector_sum = vector_sum + lax.ppermute(vector_sum, name, pairs)  30.4 us
    dot_general x4, matrix products, contract_rows(): lax.dot_general(left_op, right_op, (((0,), (0,)), ((), ())), preferred_el...  29.8 us
    pallas_call x1, Pallas kernels, attend_forward(): pl.pallas_call(forward_kernel, grid=grid, in_specs=[wide, key_rows, key_c...  21.6 us
  transfers between devices with their start and end apart: 44, of which 20 were waited for; matrix products, arithmetic and copies ran while one was open for 25% of the time, Pallas kernels for 10%

profile of v3, /device:TPU:0, one launch (start us, length us, event | category | flops | bytes accessed | tf_op | source)
XLA Modules:
  0.0 623.2 jit_solution(12952498487087321526)
XLA Ops:
  13.0 12.4 %collective-permute-done.6 = bf16[152,896]{1,0:T(8,128)(2,1)S(1)} collective-permute-done((bf16[152,896]{1,0:T(8,128)(2,1)S(1)}, bf16[152,896]{1,0:T(8,128)(2,1)S(1)}, u32[]{:S(2)}, u32[]{:S(2)}) %collective-permute-start.6) | collective-permute-done | bytes 272416 | tf_op jit(solution)/shard_map/ppermute | solution.py:26
  26.7 5.0 collective-permute-start.7
  31.7 10.9 %collective-permute-done.10 = bf16[152,896]{1,0:T(8,128)(2,1)S(1)} collective-permute-done((bf16[152,896]{1,0:T(8,128)(2,1)S(1)}, bf16[152,896]{1,0:T(8,128)(2,1)S(1)}, u32[]{:S(2)}, u32[]{:S(2)}) %collective-permute-start.10) | collective-permute-done | bytes 272416 | tf_op jit(solution)/shard_map/ppermute | solution.py:26
  42.8 9.6 %collective-permute-done.7 = bf16[2,152,896]{2,1,0:T(8,128)(2,1)} collective-permute-done((bf16[2,152,896]{2,1,0:T(8,128)(2,1)S(1)}, bf16[2,152,896]{2,1,0:T(8,128)(2,1)}, u32[]{:S(2)}, u32[]{:S(2)}) %collective-permute-start.7) | collective-permute-done | bytes 544800 | tf_op jit(solution)/shard_map/ppermute | solution.py:26
  56.3 12.2 %collective-permute-done.11 = bf16[2,152,896]{2,1,0:T(8,128)(2,1)} collective-permute-done((bf16[2,152,896]{2,1,0:T(8,128)(2,1)S(1)}, bf16[2,152,896]{2,1,0:T(8,128)(2,1)}, u32[]{:S(2)}, u32[]{:S(2)}) %collective-permute-start.11) | collective-permute-done | bytes 544800 | tf_op jit(solution)/shard_map/ppermute | solution.py:26
  72.9 11.7 %collective-permute-done.8 = bf16[2,2,152,896]{3,2,0,1:T(8,128)(2,1)} collective-permute-done((bf16[2,2,152,896]{3,2,0,1:T(8,128)(2,1)}, bf16[2,2,152,896]{3,2,0,1:T(8,128)(2,1)}, u32[]{:S(2)}, u32[]{:S(2)}) %collective-permute-start.8) | collective-permute-done | bytes 1089568 | tf_op jit(solution)/shard_map/ppermute | solution.py:26
  88.9 9.9 %collective-permute-done.12 = bf16[2,2,152,896]{3,2,1,0:T(8,128)(2,1)} collective-permute-done((bf16[2,2,152,896]{3,2,1,0:T(8,128)(2,1)}, bf16[2,2,152,896]{3,2,1,0:T(8,128)(2,1)}, u32[]{:S(2)}, u32[]{:S(2)}) %collective-permute-start.12) | collective-permute-done | bytes 1089568 | tf_op jit(solution)/shard_map/ppermute | solution.py:26
  103.5 46.9 %collective-permute-done.9 = bf16[2,2,2,152,896]{4,3,0,1,2:T(8,128)(2,1)} collective-permute-done((bf16[2,2,2,152,896]{4,3,0,1,2:T(8,128)(2,1)}, bf16[2,2,2,152,896]{4,3,0,1,2:T(8,128)(2,1)}, u32[]{:S(2)}, u32[]{:S(2)}) %collective-permute-start.9) | collective-permute-done | bytes 2179104 | tf_op jit(solution)/shard_map/ppermute | solution.py:26
  199.0 21.6 %shard_map.152 = bf16[14,64,384]{2,1,0:T(8,128)(2,1)S(1)} custom-call(bf16[14,64,384]{2,1,0:T(8,128)(2,1)S(1)} %copy.69.qt_ref, bf16[2,1536,64]{2,1,0:T(8,128)(2,1)S(1)} %get-tuple-element.48.k_ref, bf16[2,64,1536]{2,1,0:T(8,128)(2,1)S(1)} %get-tuple-element.64.vt_ref, s32[1536,1]{1,0:T(8,128)S(1)} %bitcast.228, s32[1,384]{1,0:T(1,128)S(1)} %iota_add_fusion.row_ref, ...), custom_call_target="tpu_custom_call" | custom-call | flops 8455716864 | bytes 8388608 | tf_op jit(solution)/shard_map/pallas_call | solution.py:198
  224.1 5.9 select_bitcast_fusion.1
  230.1 7.1 %pad_maximum_fusion = bf16[2,2,2,2,2,304,896]{6,5,4,3,2,1,0:T(8,128)(2,1)} fusion(bf16[2,2,1,2,2,304,896]{6,5,4,3,2,1,0:T(8,128)(2,1)S(1)} %get-tuple-element.25, bf16[2,2,1,2,2,304,896]{6,5,4,3,2,1,0:T(8,128)(2,1)S(1)} %get-tuple-element.24), kind=kLoop, calls=%fused_computation.2 | loop fusion | flops 8716288 | bytes 34865152 | tf_op jit(solution)/shard_map/stack | solution.py:30
  237.2 14.9 %fusion.55 = f32[384,9728]{1,0:T(8,128)} fusion(bf16[9728,896]{1,0:T(8,128)(2,1)} %bitcast.236, f32[384,896]{1,0:T(8,128)S(1)} %get-tuple-element.83, f32[896]{0:T(1024)S(1)} %mul.316, f32[384]{0:T(512)S(1)} %get-tuple-element.81), kind=kOutput, calls=%fused_computation.197 | convolution fusion | flops 6695141376 | bytes 33756160 | tf_op jit(solution)/shard_map/dot_general | solution.py:94
  252.1 13.9 %multiply_convert_fusion.1 = (bf16[384,4864]{1,0:T(8,128)(2,1)S(1)}, bf16[384,4864]{1,0:T(8,128)(2,1)}, bf16[384,4864]{1,0:T(8,128)(2,1)}) fusion(f32[384,9728]{1,0:T(8,128)} %fusion.55, bf16[4864,896]{1,0:T(8,128)(2,1)} %all-gather.5.cloned.1.call-done, bf16[1,384,896]{2,1,0:T(8,128)(2,1)S(1)} %copy-done.43), kind=kOutput, calls=%fused_computation.15 | convolution fusion | flops 3375071232 | bytes 35553280 | tf_op jit(solution)/shard_map/dot_general | solution.py:94
  267.8 14.7 %multiply_reduce_fusion = (f32[896]{0:T(1024)}, f32[384]{0:T(512)}, f32[384,896]{1,0:T(8,128)}) fusion(f32[384,896]{1,0:T(8,128)S(1)} %get-tuple-element.83, f32[384]{0:T(512)S(1)} %copy-done.51, f32[896]{0:T(1024)S(1)} %mul.316, bf16[9728,896]{1,0:T(8,128)(2,1)} %bitcast.237, bf16[384,4864]{1,0:T(8,128)(2,1)} %get-tuple-element.21, ...), kind=kOutput, calls=%fused_computation.83 | convolution fusion | flops 6711114240 | bytes 27666432 | tf_op jit(solution)/shard_map/dot_general | solution.py:295
  282.5 17.7 %convolution_convert_fusion = bf16[9728,896]{1,0:T(8,128)(2,1)} fusion(bf16[384,4864]{1,0:T(8,128)(2,1)} %get-tuple-element.21, bf16[384,4864]{1,0:T(8,128)(2,1)} %copy-done.57, f32[384,896]{1,0:T(8,128)S(1)} %get-tuple-element.83, f32[896]{0:T(1024)S(1)} %mul.316, f32[384]{0:T(512)} %copy-done.50), kind=kOutput, calls=%fused_computation.1 | convolution fusion | flops 6718799872 | bytes 26285056 | tf_op jit(solution)/shard_map/dot_general | solution.py:88
  308.0 11.8 %constant_dynamic-slice_fusion.7 = (bf16[2,2,1,2,2,304,896]{6,5,4,3,2,1,0:T(8,128)(2,1)}, bf16[2,2,1,2,2,304,896]{6,5,4,3,2,1,0:T(8,128)(2,1)}) fusion(bf16[2,2,2,2,2,304,896]{6,5,4,3,2,1,0:T(8,128)(2,1)} %bitcast.235, s32[]{:T(128)S(6)} %select_n.222, s32[]{:T(128)S(6)} %select_n.223), kind=kLoop, calls=%fused_computation.168 | loop fusion | bytes 34865160 | tf_op jit(solution)/shard_map/jit(dynamic_index_in_dim)/dynamic_slice | solution.py:118
  319.7 7.8 %copy.117 = bf16[2,2,1,2,2,304,896]{6,5,0,1,4,3,2:T(8,128)(2,1)} copy(bf16[2,2,1,2,2,304,896]{6,5,4,3,2,1,0:T(8,128)(2,1)} %get-tuple-element.23) | data formatting | bytes 17432576 | tf_op jit(solution)/shard_map/jit(dynamic_index_in_dim)/dynamic_slice | solution.py:117
  329.6 39.7 %shard_map.153 = (f32[14,64,384]{2,1,0:T(8,128)S(1)}, f32[2,1536,64]{2,1,0:T(8,128)}, f32[2,1536,64]{2,1,0:T(8,128)}) custom-call(bf16[14,64,384]{2,1,0:T(8,128)(2,1)S(1)} %copy-done.4, bf16[14,384,64]{2,1,0:T(8,128)(2,1)} %get-tuple-element.41.q_ref, bf16[14,64,384]{2,1,0:T(8,128)(2,1)S(1)} %bitcast.227, bf16[14,384,64]{2,1,0:T(8,128)(2,1)} %bitcast.250, ...), custom_call_target="tpu_custom_call" | custom-call | flops 21139292160 | bytes 8388608 | tf_op jit(solution)/shard_map/pallas_call | solution.py:211
  384.4 9.7 %convolution_convert_fusion.1 = bf16[4864,896]{1,0:T(8,128)(2,1)} fusion(bf16[384,4864]{1,0:T(8,128)(2,1)} %get-tuple-element.26, bf16[1,384,896]{2,1,0:T(8,128)(2,1)S(1)} %copy-done.44), kind=kOutput, calls=%fused_computation.5 | convolution fusion | flops 3351412736 | bytes 13139968 | tf_op jit(solution)/shard_map/dot_general | solution.py:88
  394.0 6.4 %constant_dynamic-slice_fusion.5 = (bf16[2,2,1,2,2,152,896]{6,5,4,3,2,1,0:T(8,128)(2,1)}, bf16[2,2,1,2,2,152,896]{6,5,4,3,2,1,0:T(8,128)(2,1)S(1)}) fusion(bf16[2,2,2,2,2,152,896]{6,5,4,3,2,1,0:T(8,128)(2,1)} %bitcast.240, s32[]{:T(128)S(6)} %select_n.222, s32[]{:T(128)S(6)} %select_n.223), kind=kLoop, calls=%fused_computation.166 | loop fusion | bytes 17432584 | tf_op jit(solution)/shard_map/jit(dynamic_index_in_dim)/dynamic_slice | solution.py:118
  424.8 16.3 %collective-permute-done.37 = f32[2,736]{1,0:T(2,128)S(1)} collective-permute-done((f32[2,736]{1,0:T(2,128)S(1)}, f32[2,736]{1,0:T(2,128)S(1)}, u32[]{:S(2)}, u32[]{:S(2)}) %collective-permute-start.37) | collective-permute-done | bytes 5920 | tf_op jit(solution)/shard_map/ppermute | solution.py:120
  447.6 4.8 fusion.1
  454.2 5.2 fusion
  462.2 7.7 %fusion.31 = bf16[1,384,896]{2,1,0:T(8,128)(2,1)} fusion(f32[384,896]{1,0:T(8,128)S(1)} %copy-done.34, bf16[384,4864]{1,0:T(8,128)(2,1)S(1)} %copy-done.56, bf16[4864,896]{1,0:T(8,128)(2,1)} %all-gather.5.cloned.1.call-done), kind=kOutput, calls=%fused_computation.90 | convolution fusion | flops 3347742720 | bytes 14516224 | tf_op jit(solution)/shard_map/dot_general | solution.py:288
  471.9 30.4 %collective-permute-done.40 = f32[736]{0:T(1024)S(1)} collective-permute-done((f32[736]{0:T(1024)S(1)}, f32[736]{0:T(1024)S(1)}, u32[]{:S(2)}, u32[]{:S(2)}) %collective-permute-start.40) | collective-permute-done | bytes 2976 | tf_op jit(solution)/shard_map/ppermute | solution.py:374
  502.3 5.9 collective-permute-start.41
  525.8 21.0 %collective-permute-done.22 = bf16[64,896]{1,0:T(8,128)(2,1)S(1)} collective-permute-done((bf16[64,896]{1,0:T(8,128)(2,1)S(1)}, bf16[64,896]{1,0:T(8,128)(2,1)S(1)}, u32[]{:S(2)}, u32[]{:S(2)}) %collective-permute-start.22) | collective-permute-done | bytes 114720 | tf_op jit(solution)/shard_map/ppermute | solution.py:120
  547.6 21.7 %collective-permute-done.34 = bf16[2,2,152,896]{3,2,0,1:T(8,128)(2,1)S(1)} collective-permute-done((bf16[2,2,152,896]{3,2,0,1:T(8,128)(2,1)S(1)}, bf16[2,2,152,896]{3,2,0,1:T(8,128)(2,1)S(1)}, u32[]{:S(2)}, u32[]{:S(2)}) %collective-permute-start.34) | collective-permute-done | bytes 1089568 | tf_op jit(solution)/shard_map/ppermute | solution.py:120
  574.0 9.1 %collective-permute-done.35 = bf16[2,152,896]{2,1,0:T(8,128)(2,1)S(1)} collective-permute-done((bf16[2,152,896]{2,1,0:T(8,128)(2,1)S(1)}, bf16[2,152,896]{2,1,0:T(8,128)(2,1)S(1)}, u32[]{:S(2)}, u32[]{:S(2)}) %collective-permute-start.35) | collective-permute-done | bytes 544800 | tf_op jit(solution)/shard_map/ppermute | solution.py:120
  584.7 5.1 collective-permute-done.26
  590.1 11.2 %collective-permute-done.30 = bf16[2,152,896]{2,1,0:T(8,128)(2,1)S(1)} collective-permute-done((bf16[2,152,896]{2,1,0:T(8,128)(2,1)S(1)}, bf16[2,152,896]{2,1,0:T(8,128)(2,1)S(1)}, u32[]{:S(2)}, u32[]{:S(2)}) %collective-permute-start.30) | collective-permute-done | bytes 544800 | tf_op jit(solution)/shard_map/ppermute | solution.py:120
  603.6 11.4 %collective-permute-done.31 = bf16[152,896]{1,0:T(8,128)(2,1)S(1)} collective-permute-done((bf16[152,896]{1,0:T(8,128)(2,1)S(1)}, bf16[152,896]{1,0:T(8,128)(2,1)S(1)}, u32[]{:S(2)}, u32[]{:S(2)}) %collective-permute-start.31) | collective-permute-done | bytes 272416 | tf_op jit(solution)/shard_map/ppermute | solution.py:120
  (343 shorter events, 168.0 us)
Async XLA Ops:
  7.2 162.0 %all-gather.3.cloned.1.call-start = ((), (), s32[]{:S(2)}) async-start(), calls=%async_computation | async-start | bytes 3784704 | tf_op jit(solution)/shard_map/all_gather | solution.py:245
  7.9 244.2 %all-gather.5.cloned.1.call-start = ((), (), s32[]{:S(2)}) async-start(), calls=%async_computation.1 | async-start | bytes 8988672 | tf_op jit(solution)/shard_map/all_gather | solution.py:247
  8.9 16.5 %collective-permute-start.6 = (bf16[152,896]{1,0:T(8,128)(2,1)S(1)}, bf16[152,896]{1,0:T(8,128)(2,1)S(1)}, u32[]{:S(2)}, u32[]{:S(2)}) collective-permute-start(bf16[152,896]{1,0:T(8,128)(2,1)S(1)} %slice.128), channel_id=1, source_target_pairs={{0,16},{4,20},{8,24},{12,28},{16,0},{20,4},{24,8},{28,12},{1,17},{... | collective-permute-start | bytes 817160 | tf_op jit(solution)/shard_map/ppermute | solution.py:26
  26.6 16.0 %collective-permute-start.10 = (bf16[152,896]{1,0:T(8,128)(2,1)S(1)}, bf16[152,896]{1,0:T(8,128)(2,1)S(1)}, u32[]{:S(2)}, u32[]{:S(2)}) collective-permute-start(bf16[152,896]{1,0:T(8,128)(2,1)S(1)} %get-tuple-element.65), channel_id=1, source_target_pairs={{0,16},{4,20},{8,24},{12,28},{16,0},{20,4},{24,8},{28,12},{1,17},{... | collective-permute-start | bytes 817160 | tf_op jit(solution)/shard_map/ppermute | solution.py:26
  26.7 25.7 %collective-permute-start.7 = (bf16[2,152,896]{2,1,0:T(8,128)(2,1)S(1)}, bf16[2,152,896]{2,1,0:T(8,128)(2,1)}, u32[]{:S(2)}, u32[]{:S(2)}) collective-permute-start(bf16[2,152,896]{2,1,0:T(8,128)(2,1)S(1)} %pad_maximum_fusion.15), channel_id=1, source_target_pairs={{0,8},{4,12},{8,0},{12,4},{16,24},{20,28},{24,16},{28,20},{1,9},{5... | collective-permute-start | bytes 1634312 | tf_op jit(solution)/shard_map/ppermute | solution.py:26
  42.7 25.7 %collective-permute-start.11 = (bf16[2,152,896]{2,1,0:T(8,128)(2,1)S(1)}, bf16[2,152,896]{2,1,0:T(8,128)(2,1)}, u32[]{:S(2)}, u32[]{:S(2)}) collective-permute-start(bf16[2,152,896]{2,1,0:T(8,128)(2,1)S(1)} %pad_maximum_fusion.16), channel_id=1, source_target_pairs={{0,8},{4,12},{8,0},{12,4},{16,24},{20,28},{24,16},{28,20},{1,9},{5... | collective-permute-start | bytes 1634312 | tf_op jit(solution)/shard_map/ppermute | solution.py:26
  54.7 29.9 %collective-permute-start.8 = (bf16[2,2,152,896]{3,2,0,1:T(8,128)(2,1)}, bf16[2,2,152,896]{3,2,0,1:T(8,128)(2,1)}, u32[]{:S(2)}, u32[]{:S(2)}) collective-permute-start(bf16[2,2,152,896]{3,2,0,1:T(8,128)(2,1)} %pad_maximum_fusion.10), channel_id=1, source_target_pairs={{0,2},{1,3},{2,0},{3,1},{4,6},{5,7},{6,4},{7,5},{8,10},{9,11},{10,... | collective-permute-start | bytes 3268616 | tf_op jit(solution)/shard_map/ppermute | solution.py:26
  71.5 27.3 %collective-permute-start.12 = (bf16[2,2,152,896]{3,2,1,0:T(8,128)(2,1)}, bf16[2,2,152,896]{3,2,1,0:T(8,128)(2,1)}, u32[]{:S(2)}, u32[]{:S(2)}) collective-permute-start(bf16[2,2,152,896]{3,2,1,0:T(8,128)(2,1)} %pad_maximum_fusion.11), channel_id=1, source_target_pairs={{0,1},{1,0},{2,3},{3,2},{4,5},{5,4},{6,7},{7,6},{8,9},{9,8},{10,11... | collective-permute-start | bytes 3268616 | tf_op jit(solution)/shard_map/ppermute | solution.py:26
  87.7 62.7 %collective-permute-start.9 = (bf16[2,2,2,152,896]{4,3,0,1,2:T(8,128)(2,1)}, bf16[2,2,2,152,896]{4,3,0,1,2:T(8,128)(2,1)}, u32[]{:S(2)}, u32[]{:S(2)}) collective-permute-start(bf16[2,2,2,152,896]{4,3,0,1,2:T(8,128)(2,1)} %pad_maximum_fusion.6), channel_id=1, source_target_pairs={{0,1},{1,0},{2,3},{3,2},{4,5},{5,4},{6,7},{7,6},{8,9},{9,8},{10,11... | collective-permute-start | bytes 6537224 | tf_op jit(solution)/shard_map/ppermute | solution.py:26
  102.1 50.4 %collective-permute-start.13 = (bf16[2,2,2,152,896]{4,3,2,1,0:T(8,128)(2,1)}, bf16[2,2,2,152,896]{4,3,2,1,0:T(8,128)(2,1)}, u32[]{:S(2)}, u32[]{:S(2)}) collective-permute-start(bf16[2,2,2,152,896]{4,3,2,1,0:T(8,128)(2,1)} %pad_maximum_fusion.7), channel_id=1, source_target_pairs={{0,2},{1,3},{2,0},{3,1},{4,6},{5,7},{6,4},{7,5},{8,10},{9,11},{10,... | collective-permute-start | bytes 6537224 | tf_op jit(solution)/shard_map/ppermute | solution.py:26
  160.9 62.6 %collective-permute-start.14 = (bf16[2,2,2,2,304,896]{5,4,3,2,1,0:T(8,128)(2,1)}, bf16[2,2,2,2,304,896]{5,4,3,2,1,0:T(8,128)(2,1)}, u32[]{:S(2)}, u32[]{:S(2)}) collective-permute-start(bf16[2,2,2,2,304,896]{5,4,3,2,1,0:T(8,128)(2,1)} %maximum_maximum_fusion), channel_id=1, source_target_pairs={{0,4},{4,0},{8,12},{12,8},{16,20},{20,16},{24,28},{28,24},{1,5},{5... | collective-permute-start | bytes 26148872 | tf_op jit(solution)/shard_map/ppermute | solution.py:26
  174.4 16.6 %collective-permute-start.3 = (bf16[384,256]{1,0:T(8,128)(2,1)}, bf16[384,256]{1,0:T(8,128)(2,1)}, u32[]{:S(2)}, u32[]{:S(2)}) collective-permute-start(bf16[384,256]{1,0:T(8,128)(2,1)} %pad_maximum_fusion.17), channel_id=1, source_target_pairs={{0,1},{1,0},{2,3},{3,2},{4,5},{5,4},{6,7},{7,6},{8,9},{9,8},{10,11... | collective-permute-start | bytes 589832 | tf_op jit(solution)/shard_map/ppermute | solution.py:135
  327.5 126.6 %collective-permute-start.23 = (bf16[2,2,2,2,304,896]{5,4,0,1,3,2:T(8,128)(2,1)}, bf16[2,2,2,2,304,896]{5,4,0,1,3,2:T(8,128)(2,1)}, u32[]{:S(2)}, u32[]{:S(2)}) collective-permute-start(bf16[2,2,2,2,304,896]{5,4,0,1,3,2:T(8,128)(2,1)} %bitcast.239), channel_id=1, source_target_pairs={{0,4},{4,0},{8,12},{12,8},{16,20},{20,16},{24,28},{28,24},{1,5},{5... | collective-permute-start | bytes 26148872 | tf_op jit(solution)/shard_map/ppermute | solution.py:120
  380.8 23.1 %collective-permute-start.15 = (bf16[384,256]{0,1:T(8,128)(2,1)S(1)}, bf16[384,256]{0,1:T(8,128)(2,1)S(1)}, u32[]{:S(2)}, u32[]{:S(2)}) collective-permute-start(bf16[384,256]{0,1:T(8,128)(2,1)S(1)} %bitcast.259), channel_id=1, source_target_pairs={{0,1},{1,0},{2,3},{3,2},{4,5},{5,4},{6,7},{7,6},{8,9},{9,8},{10,11... | collective-permute-start | bytes 589832 | tf_op jit(solution)/shard_map/ppermute | solution.py:322
  381.7 22.3 %collective-permute-start.16 = (bf16[384,256]{0,1:T(8,128)(2,1)S(1)}, bf16[384,256]{0,1:T(8,128)(2,1)S(1)}, u32[]{:S(2)}, u32[]{:S(2)}) collective-permute-start(bf16[384,256]{0,1:T(8,128)(2,1)S(1)} %bitcast.258), channel_id=1, source_target_pairs={{0,2},{1,3},{2,0},{3,1},{4,6},{5,7},{6,4},{7,5},{8,10},{9,11},{10,... | collective-permute-start | bytes 589832 | tf_op jit(solution)/shard_map/ppermute | solution.py:322
  383.0 20.9 %collective-permute-start.17 = (bf16[384,256]{0,1:T(8,128)(2,1)S(1)}, bf16[384,256]{0,1:T(8,128)(2,1)S(1)}, u32[]{:S(2)}, u32[]{:S(2)}) collective-permute-start(bf16[384,256]{0,1:T(8,128)(2,1)S(1)} %bitcast.257), channel_id=1, source_target_pairs={{0,3},{1,2},{2,1},{3,0},{4,7},{5,6},{6,5},{7,4},{8,11},{9,10},{10,... | collective-permute-start | bytes 589832 | tf_op jit(solution)/shard_map/ppermute | solution.py:322
  402.8 44.8 %collective-permute-start.32 = (bf16[2,2,2,2,152,896]{5,4,2,3,0,1:T(8,128)(2,1)}, bf16[2,2,2,2,152,896]{5,4,2,3,0,1:T(8,128)(2,1)}, u32[]{:S(2)}, u32[]{:S(2)}) collective-permute-start(bf16[2,2,2,2,152,896]{5,4,2,3,0,1:T(8,128)(2,1)} %bitcast.223), channel_id=1, source_target_pairs={{0,4},{4,0},{8,12},{12,8},{16,20},{20,16},{24,28},{28,24},{1,5},{5... | collective-permute-start | bytes 13074440 | tf_op jit(solution)/shard_map/ppermute | solution.py:120
  418.2 26.7 %collective-permute-start.19 = (bf16[2,2,2,64,896]{4,3,0,1,2:T(8,128)(2,1)}, bf16[2,2,2,64,896]{4,3,0,1,2:T(8,128)(2,1)}, u32[]{:S(2)}, u32[]{:S(2)}) collective-permute-start(bf16[2,2,2,64,896]{4,3,0,1,2:T(8,128)(2,1)} %dynamic-slice_bitcast_fusion.6), channel_id=1, source_target_pairs={{0,1},{1,0},{2,3},{3,2},{4,5},{5,4},{6,7},{7,6},{8,9},{9,8},{10,11... | collective-permute-start | bytes 2752520 | tf_op jit(solution)/shard_map/ppermute | solution.py:120
  423.5 17.6 %collective-permute-start.37 = (f32[2,736]{1,0:T(2,128)S(1)}, f32[2,736]{1,0:T(2,128)S(1)}, u32[]{:S(2)}, u32[]{:S(2)}) collective-permute-start(f32[2,736]{1,0:T(2,128)S(1)} %bitcast.261), channel_id=1, source_target_pairs={{0,1},{1,0},{2,3},{3,2},{4,5},{5,4},{6,7},{7,6},{8,9},{9,8},{10,11... | collective-permute-start | bytes 17672 | tf_op jit(solution)/shard_map/ppermute | solution.py:120
  444.9 25.0 %collective-permute-start.39 = (f32[736]{0:T(1024)S(1)}, f32[736]{0:T(1024)S(1)}, u32[]{:S(2)}, u32[]{:S(2)}) collective-permute-start(f32[736]{0:T(1024)S(1)} %add.343), channel_id=1, source_target_pairs={{0,4},{4,0},{8,12},{12,8},{16,20},{20,16},{24,28},{28,24},{1,5},{5... | collective-permute-start | bytes 8840 | tf_op jit(solution)/shard_map/ppermute | solution.py:374
  446.7 61.6 %collective-permute-start.20 = (bf16[2,2,64,896]{3,2,0,1:T(8,128)(2,1)S(1)}, bf16[2,2,64,896]{3,2,0,1:T(8,128)(2,1)S(1)}, u32[]{:S(2)}, u32[]{:S(2)}) collective-permute-start(bf16[2,2,64,896]{3,2,0,1:T(8,128)(2,1)S(1)} %dynamic-slice_bitcast_fusion.10), channel_id=1, source_target_pairs={{0,2},{1,3},{2,0},{3,1},{4,6},{5,7},{6,4},{7,5},{8,10},{9,11},{10,... | collective-permute-start | bytes 1376264 | tf_op jit(solution)/shard_map/ppermute | solution.py:120
  452.6 63.4 %collective-permute-start.33 = (bf16[2,2,2,152,896]{4,3,1,2,0:T(8,128)(2,1)S(1)}, bf16[2,2,2,152,896]{4,3,1,2,0:T(8,128)(2,1)}, u32[]{:S(2)}, u32[]{:S(2)}) collective-permute-start(bf16[2,2,2,152,896]{4,3,1,2,0:T(8,128)(2,1)S(1)} %dynamic-slice_bitcast_fusion), channel_id=1, source_target_pairs={{0,8},{4,12},{8,0},{12,4},{16,24},{20,28},{24,16},{28,20},{1,9},{5... | collective-permute-start | bytes 6537224 | tf_op jit(solution)/shard_map/ppermute | solution.py:120
  460.8 60.2 %collective-permute-start.24 = (bf16[2,2,2,152,896]{4,3,0,1,2:T(8,128)(2,1)S(1)}, bf16[2,2,2,152,896]{4,3,0,1,2:T(8,128)(2,1)S(1)}, u32[]{:S(2)}, u32[]{:S(2)}) collective-permute-start(bf16[2,2,2,152,896]{4,3,0,1,2:T(8,128)(2,1)S(1)} %dynamic-slice_bitcast_fusion.2), channel_id=1, source_target_pairs={{0,1},{1,0},{2,3},{3,2},{4,5},{5,4},{6,7},{7,6},{8,9},{9,8},{10,11... | collective-permute-start | bytes 6537224 | tf_op jit(solution)/shard_map/ppermute | solution.py:120
  469.9 32.4 %collective-permute-start.40 = (f32[736]{0:T(1024)S(1)}, f32[736]{0:T(1024)S(1)}, u32[]{:S(2)}, u32[]{:S(2)}) collective-permute-start(f32[736]{0:T(1024)S(1)} %add.344), channel_id=1, source_target_pairs={{0,8},{4,12},{8,0},{12,4},{16,24},{20,28},{24,16},{28,20},{1,9},{5... | collective-permute-start | bytes 8840 | tf_op jit(solution)/shard_map/ppermute | solution.py:374
  471.1 52.0 %collective-permute-start.28 = (bf16[2,2,2,152,896]{4,3,0,1,2:T(8,128)(2,1)S(1)}, bf16[2,2,2,152,896]{4,3,0,1,2:T(8,128)(2,1)S(1)}, u32[]{:S(2)}, u32[]{:S(2)}) collective-permute-start(bf16[2,2,2,152,896]{4,3,0,1,2:T(8,128)(2,1)S(1)} %dynamic-slice_bitcast_fusion.1), channel_id=1, source_target_pairs={{0,2},{1,3},{2,0},{3,1},{4,6},{5,7},{6,4},{7,5},{8,10},{9,11},{10,... | collective-permute-start | bytes 6537224 | tf_op jit(solution)/shard_map/ppermute | solution.py:120
  515.6 31.3 %collective-permute-start.22 = (bf16[64,896]{1,0:T(8,128)(2,1)S(1)}, bf16[64,896]{1,0:T(8,128)(2,1)S(1)}, u32[]{:S(2)}, u32[]{:S(2)}) collective-permute-start(bf16[64,896]{1,0:T(8,128)(2,1)S(1)} %dynamic-slice_bitcast_fusion.15), channel_id=1, source_target_pairs={{0,16},{4,20},{8,24},{12,28},{16,0},{20,4},{24,8},{28,12},{1,17},{... | collective-permute-start | bytes 344072 | tf_op jit(solution)/shard_map/ppermute | solution.py:120
  518.3 51.0 %collective-permute-start.34 = (bf16[2,2,152,896]{3,2,0,1:T(8,128)(2,1)S(1)}, bf16[2,2,152,896]{3,2,0,1:T(8,128)(2,1)S(1)}, u32[]{:S(2)}, u32[]{:S(2)}) collective-permute-start(bf16[2,2,152,896]{3,2,0,1:T(8,128)(2,1)S(1)} %dynamic-slice_bitcast_fusion.3), channel_id=1, source_target_pairs={{0,16},{4,20},{8,24},{12,28},{16,0},{20,4},{24,8},{28,12},{1,17},{... | collective-permute-start | bytes 3268616 | tf_op jit(solution)/shard_map/ppermute | solution.py:120
  521.6 49.6 %collective-permute-start.25 = (bf16[2,2,152,896]{3,2,0,1:T(8,128)(2,1)S(1)}, bf16[2,2,152,896]{3,2,0,1:T(8,128)(2,1)S(1)}, u32[]{:S(2)}, u32[]{:S(2)}) collective-permute-start(bf16[2,2,152,896]{3,2,0,1:T(8,128)(2,1)S(1)} %dynamic-slice_bitcast_fusion.5), channel_id=1, source_target_pairs={{0,2},{1,3},{2,0},{3,1},{4,6},{5,7},{6,4},{7,5},{8,10},{9,11},{10,... | collective-permute-start | bytes 3268616 | tf_op jit(solution)/shard_map/ppermute | solution.py:120
  523.8 47.8 %collective-permute-start.29 = (bf16[2,2,152,896]{3,2,0,1:T(8,128)(2,1)S(1)}, bf16[2,2,152,896]{3,2,0,1:T(8,128)(2,1)S(1)}, u32[]{:S(2)}, u32[]{:S(2)}) collective-permute-start(bf16[2,2,152,896]{3,2,0,1:T(8,128)(2,1)S(1)} %dynamic-slice_bitcast_fusion.4), channel_id=1, source_target_pairs={{0,1},{1,0},{2,3},{3,2},{4,5},{5,4},{6,7},{7,6},{8,9},{9,8},{10,11... | collective-permute-start | bytes 3268616 | tf_op jit(solution)/shard_map/ppermute | solution.py:120
  571.5 18.3 %collective-permute-start.26 = (bf16[2,152,896]{2,1,0:T(8,128)(2,1)S(1)}, bf16[2,152,896]{2,1,0:T(8,128)(2,1)S(1)}, u32[]{:S(2)}, u32[]{:S(2)}) collective-permute-start(bf16[2,152,896]{2,1,0:T(8,128)(2,1)S(1)} %dynamic-slice_bitcast_fusion.9), channel_id=1, source_target_pairs={{0,8},{4,12},{8,0},{12,4},{16,24},{20,28},{24,16},{28,20},{1,9},{5... | collective-permute-start | bytes 1634312 | tf_op jit(solution)/shard_map/ppermute | solution.py:120
  572.0 29.3 %collective-permute-start.30 = (bf16[2,152,896]{2,1,0:T(8,128)(2,1)S(1)}, bf16[2,152,896]{2,1,0:T(8,128)(2,1)S(1)}, u32[]{:S(2)}, u32[]{:S(2)}) collective-permute-start(bf16[2,152,896]{2,1,0:T(8,128)(2,1)S(1)} %dynamic-slice_bitcast_fusion.8), channel_id=1, source_target_pairs={{0,8},{4,12},{8,0},{12,4},{16,24},{20,28},{24,16},{28,20},{1,9},{5... | collective-permute-start | bytes 1634312 | tf_op jit(solution)/shard_map/ppermute | solution.py:120
  583.3 19.0 %collective-permute-start.36 = (bf16[152,896]{1,0:T(8,128)(2,1)S(1)}, bf16[152,896]{1,0:T(8,128)(2,1)S(1)}, u32[]{:S(2)}, u32[]{:S(2)}) collective-permute-start(bf16[152,896]{1,0:T(8,128)(2,1)S(1)} %dynamic-slice_bitcast_fusion.11), channel_id=1, source_target_pairs={{0,2},{1,3},{2,0},{3,1},{4,6},{5,7},{6,4},{7,5},{8,10},{9,11},{10,... | collective-permute-start | bytes 817160 | tf_op jit(solution)/shard_map/ppermute | solution.py:120
  (73 other events, 665.8 us)
Sparse Core Ops, SparseCore 0:
  10.9 74.5 all-gather.2
  103.6 92.2 all-gather.4
